TPU v7x, 32 devices: a whole 2x2x4 slice. The times are simulated.
32 devices in a mesh: gx: 8 (over z, x), gy: 4 (over y, core).
Axes of the slice: x: 2, y: 2, z: 4, core: 2. Of those that a mesh axis runs over, the one named last changes fastest.
Arguments:
- hidden_in: bfloat16 [16, 5120], P(None, 'gx'), may hold values from -60 to 60
- norm1_gain: float32 [5120], P('gx'), may hold values from 0.1 to 1.9
- norm1_bias: float32 [5120], P('gx'), may hold values from -4 to 4
- norm2_gain: float32 [5120], P('gx'), may hold values from 0.1 to 1.9
- norm2_bias: float32 [5120], P('gx'), may hold values from -4 to 4
- w_qkv: bfloat16 [5120, 15360], P('gx', 'gy'), may hold values from -0.078125 to 0.078125
- b_qkv: float32 [15360], P('gy'), may hold values from -4 to 4
- w_out: bfloat16 [5120, 5120], P('gy', 'gx'), may hold values from -0.078125 to 0.078125
- b_out: float32 [5120], P('gx'), may hold values from -4 to 4
- w_up: bfloat16 [5120, 20480], P('gx', 'gy'), may hold values from -0.078125 to 0.078125
- b_up: float32 [20480], P('gy'), may hold values from -4 to 4
- w_down: bfloat16 [20480, 5120], P('gy', 'gx'), may hold values from -0.0390625 to 0.0390625
- b_down: float32 [5120], P('gx'), may hold values from -4 to 4
- key_cache: bfloat16 [16, 40, 1024, 128], P('gx', 'gy'), may hold values from -70 to 70
- value_cache: bfloat16 [16, 40, 1024, 128], P('gx', 'gy'), may hold values from -6 to 6
- lengths: int32 [16], replicated, may hold values from 1 to 1024, 8192 in all
- assignment: int32 [16], replicated, may hold values from 0 to 15, each once
Outputs:
- hidden_out: bfloat16 [16, 5120], P(None, 'gx')
- new_keys: bfloat16 [16, 40, 1024, 128], P('gx', 'gy')
- new_values: bfloat16 [16, 40, 1024, 128], P('gx', 'gy')
Inputs may be any that keep to these rules, and one draw needn't show every extreme that they name: `lengths`: each request's length, the largest exactly 1024. `assignment`: a permutation: every slot holds exactly one request.
All inputs are finite; a program needn't handle non-finite values.
Results may differ from a plain program's by a relative error of at most 0.0068.
Values may be sent and summed in bfloat16 or wider, within the bound.
A program may use at most 128 MiB of HBM per device.

v0:
```python
import jax
import jax.numpy as jnp
from jax import lax
from jax.sharding import PartitionSpec as P

D = 5120
HD = 128
ROT = 32


def rotate(tensor, position):
    half_rot = ROT // 2
    frequency = 10000.0 ** (-2.0 * jnp.arange(half_rot, dtype=jnp.float32) / ROT)
    angle = position.astype(jnp.float32)[:, None, None] * frequency
    cosine = jnp.cos(angle)
    sine = jnp.sin(angle)
    first_half = tensor[..., :half_rot]
    second_half = tensor[..., half_rot:ROT]
    return jnp.concatenate(
        [
            first_half * cosine - second_half * sine,
            second_half * cosine + first_half * sine,
            tensor[..., ROT:],
        ],
        axis=-1,
    )


def block_scores(query, keys, my_len):
    span_len = keys.shape[2]
    scores = jnp.einsum("shd,shpd->shp", query, keys, preferred_element_type=jnp.float32) * HD ** (
        -0.5
    )
    places = lax.iota(jnp.int32, span_len)
    valid = places[None, None, :] < my_len[:, None, None]
    return (jnp.where(valid, scores, -1e30), valid)


def on_device(
    hidden_in,
    norm1_gain,
    norm1_bias,
    norm2_gain,
    norm2_bias,
    w_qkv,
    b_qkv,
    w_out,
    b_out,
    w_up,
    b_up,
    w_down,
    b_down,
    key_cache,
    value_cache,
    lengths,
    assignment,
):
    requests = hidden_in.shape[0]
    rows_dev = key_cache.shape[0]
    heads_dev = key_cache.shape[1]
    wide_in = hidden_in.astype(jnp.float32)
    sum_rows, sum_squares = lax.psum(
        (jnp.sum(wide_in, axis=1), jnp.sum(wide_in * wide_in, axis=1)), "gx"
    )
    row_mean = sum_rows / D
    row_var = sum_squares / D - row_mean * row_mean
    normed = (wide_in - row_mean[:, None]) * lax.rsqrt(row_var + 1e-05)[:, None]
    attn_in = (normed * norm1_gain + norm1_bias).astype(jnp.bfloat16)
    mlp_in = (normed * norm2_gain + norm2_bias).astype(jnp.bfloat16)
    slot_ids = lax.iota(jnp.int32, requests)
    matches = assignment[:, None] == slot_ids[None, :]
    to_request = matches.astype(jnp.float32)
    attn_slot = jnp.dot(
        matches.T.astype(jnp.bfloat16), attn_in, preferred_element_type=jnp.float32
    ).astype(jnp.bfloat16)
    slot_len = jnp.sum(jnp.where(matches, lengths[:, None], 0), axis=0)
    my_len = lax.dynamic_slice_in_dim(slot_len, lax.axis_index("gx") * rows_dev, rows_dev, 0)
    qkv = (
        lax.psum_scatter(
            jnp.dot(attn_slot, w_qkv, preferred_element_type=jnp.float32),
            "gx",
            scatter_dimension=0,
            tiled=True,
        )
        + b_qkv
    )
    qkv = qkv.reshape(rows_dev, heads_dev, 3, HD)
    position = my_len - 1
    query = rotate(qkv[:, :, 0], position).astype(jnp.bfloat16)
    new_key = rotate(qkv[:, :, 1], position).astype(jnp.bfloat16)
    new_value = qkv[:, :, 2].astype(jnp.bfloat16)
    new_keys = key_cache
    new_values = value_cache
    zero_index = jnp.int32(0)
    for local_slot in range(rows_dev):
        slot_index = jnp.int32(local_slot)
        new_keys = lax.dynamic_update_slice(
            new_keys,
            new_key[local_slot][None, :, None, :],
            (slot_index, zero_index, position[local_slot], zero_index),
        )
        new_values = lax.dynamic_update_slice(
            new_values,
            new_value[local_slot][None, :, None, :],
            (slot_index, zero_index, position[local_slot], zero_index),
        )
    scores, valid = block_scores(query, new_keys, my_len)
    top_score = jnp.max(scores, axis=2)
    weights = jnp.where(valid, jnp.exp(scores - top_score[:, :, None]), 0.0)
    total = jnp.sum(weights, axis=2)
    weights_low = weights.astype(jnp.bfloat16)
    weighted = jnp.einsum(
        "shp,shpd->shd", weights_low, new_values, preferred_element_type=jnp.float32
    )
    attended = (weighted / total[:, :, None]).astype(jnp.bfloat16).reshape(rows_dev, heads_dev * HD)
    slot_part = jnp.dot(
        lax.all_gather(attended, "gx", axis=0, tiled=True),
        w_out,
        preferred_element_type=jnp.float32,
    )
    attn_part = jnp.dot(to_request, slot_part, precision=lax.Precision.HIGHEST)
    up_partial = jnp.dot(mlp_in, w_up, preferred_element_type=jnp.float32)
    up = lax.psum(up_partial, "gx") + b_up
    hidden = jax.nn.gelu(up, approximate=False).astype(jnp.bfloat16)
    mlp_part = jnp.dot(hidden, w_down, preferred_element_type=jnp.float32)
    branches = lax.psum(attn_part + mlp_part, "gy")
    hidden_out = (wide_in + branches + b_out + b_down).astype(jnp.bfloat16)
    return (hidden_out, new_keys, new_values)


def solution(mesh):
    return jax.shard_map(
        on_device,
        mesh=mesh,
        in_specs=(
            P(None, "gx"),
            P("gx"),
            P("gx"),
            P("gx"),
            P("gx"),
            P("gx", "gy"),
            P("gy"),
            P("gy", "gx"),
            P("gx"),
            P("gx", "gy"),
            P("gy"),
            P("gy", "gx"),
            P("gx"),
            P("gx", "gy", None, None),
            P("gx", "gy", None, None),
            P(),
            P(),
        ),
        out_specs=(P(None, "gx"), P("gx", "gy", None, None), P("gx", "gy", None, None)),
        check_vma=False,
    )
```

profile of v0, /device:TPU:0, one launch (start us, length us, event | category | flops | bytes accessed | tf_op | source)
XLA Modules:
  0.0 185.4 jit_solution(5129864537161130326)
XLA Ops:
  7.2 0.0 copy-start
  7.2 0.0 all-reduce.5.cloned.1.call-start
  7.2 0.0 copy-start.1
  7.2 5.5 %copy.67 = bf16[2,10,1024,128]{3,2,1,0:T(8,128)(2,1)} copy(bf16[2,10,1024,128]{3,2,1,0:T(8,128)(2,1)} %param.31) | data formatting | bytes 10485760
  12.7 0.0 copy-done.1
  12.7 0.0 copy-start.2
  12.7 0.0 copy-start.4
  12.7 0.0 copy-start.5
  12.7 2.4 %copy.66 = bf16[2,10,1024,128]{3,2,1,0:T(8,128)(2,1)} copy(bf16[2,10,1024,128]{3,2,1,0:T(8,128)(2,1)S(1)} %copy-done.1) | data formatting | bytes 10485760
  15.1 0.0 copy-done.2
  15.1 0.0 copy-start.6
  15.1 0.0 copy-start.7
  15.1 0.1 convert_reduce_fusion
  15.2 23.1 %all-reduce.1 = (f32[16]{0:T(128)S(1)}, f32[16]{0:T(128)S(1)}) all-reduce(f32[16]{0:T(128)S(1)} %get-tuple-element.4, f32[16]{0:T(128)S(1)} %get-tuple-element.3), channel_id=1, replica_groups=mesh['gx'=8,'gy'=4] {'gx'}, use_global_device_ids=true, to_apply=%region_4.5 | all-reduce | flops 32 | bytes 256 | tf_op jit(solution)/shard_map/psum | solution.py:62
  38.4 0.0 copy-done.4
  38.4 0.0 copy-done.5
  38.4 0.0 copy-start.13
  38.4 0.0 copy-start.14
  38.4 0.0 copy-start.3
  38.4 4.6 %fusion.63 = f32[16,5120]{1,0:T(8,128)} fusion(bf16[640,5120]{1,0:T(8,128)(2,1)} %param.26, bf16[16,640]{1,0:T(8,128)(2,1)S(1)} %copy-done.2, f32[640]{0:T(1024)S(1)} %copy-done.4, f32[640]{0:T(1024)S(1)} %copy-done.5, f32[16]{0:T(128)S(1)} %get-tuple-element.30, f32[16]{0:T(128)S(1)} %get-tuple-element.29), kind=kOutput, calls=%fused_computation.79 | convolution fusion | flops 104919040 | bytes 6907008 | tf_op jit(solution)/shard_map/dot_general | solution.py:122
  43.0 0.0 copy-done.6
  43.0 0.0 copy-done.7
  43.0 0.0 copy-done.10
  43.0 4.1 %fusion.4 = f32[16,3840]{1,0:T(8,128)} fusion(bf16[640,3840]{1,0:T(8,128)(2,1)} %param.22, bf16[16,640]{1,0:T(8,128)(2,1)S(1)} %copy-done.2, f32[640]{0:T(1024)S(1)} %copy-done.6, f32[640]{0:T(1024)S(1)} %copy-done.7, f32[16]{0:T(128)S(1)} %get-tuple-element.30, f32[16]{0:T(128)S(1)} %get-tuple-element.29, s32[16]{0:T(128)S(1)} %copy-done.10), kind=kOutput, calls=%fused_computation.6 | convolution fusion | flops 79042816 | bytes 5186752 | tf_op jit(solution)/shard_map/dot_general | solution.py:80
  47.1 0.0 all-reduce.5.cloned.1.call-update
  47.1 0.0 copy-done.13
  47.2 0.1 select_reduce_fusion
  47.2 0.1 fusion.118
  47.3 0.7 fusion.122
  50.6 0.0 copy-done.14
  50.7 0.6 dynamic-slice
  53.2 0.1 multiply_cosine_fusion
  53.3 0.1 iota_compare_fusion
  53.4 63.8 %all-reduce.5.cloned.1.call-done = (f32[16,3840]{1,0:T(8,128)}, f32[16,5120]{1,0:T(8,128)}) async-done(((f32[16,3840]{1,0:T(8,128)}, f32[16,5120]{1,0:T(8,128)}), (f32[16,3840]{1,0:T(8,128)}, f32[16,5120]{1,0:T(8,128)})) %all-reduce.5.cloned.1.call-update) | async-done | bytes 573456
  117.2 0.0 copy-done.3
  117.2 0.9 dynamic-slice_add_fusion
  118.3 0.1 slice.90
  118.4 0.1 slice.91
  118.5 0.1 subtract_convert_fusion.1
  118.6 0.1 pad_maximum_fusion
  118.7 1.4 dynamic_update_slice.12
  120.0 0.1 maximum_bitcast_fusion
  120.1 1.4 dynamic_update_slice.13
  121.5 3.9 %fusion.80 = f32[2,10,1,1024]{3,2,1,0:T(1,128)S(1)} fusion(bf16[2,10,1024,128]{3,2,1,0:T(8,128)(2,1)} %dynamic_update_slice.13, bf16[2,10,128,1]{2,0,1,3:T(2,128)(2,1)S(1)} %maximum_bitcast_fusion), kind=kOutput, calls=%fused_computation.92 | convolution fusion | flops 5242880 | bytes 5329920 | tf_op jit(solution)/shard_map/shd,shpd->shp/dot_general | solution.py:31
  125.4 0.2 fusion.3
  125.6 0.1 fusion.119
  125.7 0.1 copy.42
  125.8 1.4 dynamic_update_slice.14
  127.2 1.4 dynamic_update_slice.15
  128.5 3.3 %fusion.48 = f32[2,10,1,128]{3,2,1,0:T(1,128)S(1)} fusion(bf16[2,10,1024,128]{3,2,1,0:T(8,128)(2,1)} %dynamic_update_slice.15, bf16[2,10,1024,1]{2,0,1,3:T(2,128)(2,1)S(1)} %get-tuple-element.12), kind=kOutput, calls=%fused_computation.59 | convolution fusion | flops 5242880 | bytes 5294080 | tf_op jit(solution)/shard_map/shp,shpd->shd/dot_general | solution.py:112
  131.8 0.1 fusion.79
  131.9 30.6 %all-gather = bf16[8,2,1280]{2,1,0:T(2,128)(2,1)S(1)} all-gather(bf16[1,2,1280]{2,1,0:T(2,128)(2,1)S(1)} %reshape.113), channel_id=1, replica_groups=mesh['gx'=8,'gy'=4] {'gx'}, dimensions={0}, use_global_device_ids=true | all-gather | bytes 46080 | tf_op jit(solution)/shard_map/all_gather | solution.py:117
  162.5 0.0 copy-done
  162.5 0.3 fusion.123
  162.8 0.2 fusion.82
  163.1 0.0 copy-done.11
  163.1 0.0 copy-done.12
  163.1 0.0 copy-start.8
  163.1 0.0 copy-start.9
  163.1 4.3 %convolution_add_fusion = f32[16,640]{1,0:T(8,128)S(1)} fusion(f32[16,640]{1,0:T(8,128)S(1)} %fusion.82, bf16[5120,640]{1,0:T(8,128)(2,1)} %param.28, f32[16,5120]{1,0:T(8,128)S(1)} %copy-done.11, f32[5120]{0:T(1024)S(1)} %copy-done.12), kind=kOutput, calls=%fused_computation.4 | convolution fusion | flops 110274560 | bytes 6983680 | tf_op jit(solution)/shard_map/dot_general | solution.py:125
  167.4 10.5 %psum.31 = f32[16,640]{1,0:T(8,128)S(1)} all-reduce(f32[16,640]{1,0:T(8,128)S(1)} %convolution_add_fusion), channel_id=1, replica_groups=mesh['gx'=8,'gy'=4] {'gy'}, use_global_device_ids=true, to_apply=%region_9.10 | all-reduce | flops 10240 | bytes 81920 | tf_op jit(solution)/shard_map/psum | solution.py:126
  177.9 0.0 copy-done.8
  177.9 0.0 copy-done.9
  177.9 0.6 fusion.60
  (14 shorter events, 0.2 us)
Async XLA Ops:
  7.2 155.3 %copy-start = (bf16[1280,640]{1,0:T(8,128)(2,1)S(1)}, bf16[1280,640]{1,0:T(8,128)(2,1)}, u32[]{:S(2)}) copy-start(bf16[1280,640]{1,0:T(8,128)(2,1)} %param.24) | copy-start | bytes 4915204
  7.2 110.1 %all-reduce.5.cloned.1.call-start = ((), (), s32[]{:S(2)}) async-start(), calls=%async_computation | async-start | bytes 1146880
  7.2 5.5 %copy-start.1 = (bf16[2,10,1024,128]{3,2,1,0:T(8,128)(2,1)S(1)}, bf16[2,10,1024,128]{3,2,1,0:T(8,128)(2,1)}, u32[]{:S(2)}) copy-start(bf16[2,10,1024,128]{3,2,1,0:T(8,128)(2,1)} %param.30) | copy-start | bytes 15728644
  12.7 2.4 %copy-start.2 = (bf16[16,640]{1,0:T(8,128)(2,1)S(1)}, bf16[16,640]{1,0:T(8,128)(2,1)}, u32[]{:S(2)}) copy-start(bf16[16,640]{1,0:T(8,128)(2,1)} %param.17) | copy-start | bytes 61444
  12.7 25.6 %copy-start.4 = (f32[640]{0:T(1024)S(1)}, f32[640]{0:T(1024)}, u32[]{:S(2)}) copy-start(f32[640]{0:T(1024)} %param.21) | copy-start | bytes 7684
  12.7 25.6 %copy-start.5 = (f32[640]{0:T(1024)S(1)}, f32[640]{0:T(1024)}, u32[]{:S(2)}) copy-start(f32[640]{0:T(1024)} %param.20) | copy-start | bytes 7684
  15.1 27.9 %copy-start.6 = (f32[640]{0:T(1024)S(1)}, f32[640]{0:T(1024)}, u32[]{:S(2)}) copy-start(f32[640]{0:T(1024)} %param.19) | copy-start | bytes 7684
  15.1 27.9 %copy-start.7 = (f32[640]{0:T(1024)S(1)}, f32[640]{0:T(1024)}, u32[]{:S(2)}) copy-start(f32[640]{0:T(1024)} %param.18) | copy-start | bytes 7684
  15.1 27.9 %copy-start.10 = (s32[16]{0:T(128)S(1)}, s32[16]{0:T(128)}, u32[]{:S(2)}) copy-start(s32[16]{0:T(128)} %param.33) | copy-start | bytes 196
  38.4 8.8 %copy-start.13 = (s32[16]{0:T(128)S(1)}, s32[16]{0:T(128)}, u32[]{:S(2)}) copy-start(s32[16]{0:T(128)} %param.32) | copy-start | bytes 196
  38.4 12.3 %copy-start.14 = (u32[32]{0:T(128)S(1)}, u32[32]{0:T(128)}, u32[]{:S(2)}) copy-start(u32[32]{0:T(128)} %constant.103) | copy-start | bytes 388
  38.4 78.9 %copy-start.3 = (f32[3840]{0:T(1024)S(1)}, f32[3840]{0:T(1024)}, u32[]{:S(2)}) copy-start(f32[3840]{0:T(1024)} %param.23) | copy-start | bytes 46084
  125.4 37.6 %copy-start.11 = (f32[16,5120]{1,0:T(8,128)S(1)}, f32[16,5120]{1,0:T(8,128)}, u32[]{:S(2)}) copy-start(f32[16,5120]{1,0:T(8,128)} %get-tuple-element.8) | copy-start | bytes 983044
  125.4 37.6 %copy-start.12 = (f32[5120]{0:T(1024)S(1)}, f32[5120]{0:T(1024)}, u32[]{:S(2)}) copy-start(f32[5120]{0:T(1024)} %param.27) | copy-start | bytes 61444
  163.1 14.8 %copy-start.8 = (f32[640]{0:T(1024)S(1)}, f32[640]{0:T(1024)}, u32[]{:S(2)}) copy-start(f32[640]{0:T(1024)} %param.29) | copy-start | bytes 7684
  163.1 14.8 %copy-start.9 = (f32[640]{0:T(1024)S(1)}, f32[640]{0:T(1024)}, u32[]{:S(2)}) copy-start(f32[640]{0:T(1024)} %param.25) | copy-start | bytes 7684
Sparse Core Ops, SparseCore 0:
  47.3 69.9 all-reduce.4
where the time goes:
time: 186 us; the launch traced here: 185 us
  blocking collectives  64.2 us (35%)
  waiting for transfers between devices  63.8 us (34%)
  matrix products  20.7 us (11%)
  between operations  18.9 us (10%)
  local copies, waits for them, and re-layouts  15 us (8%)
  other arithmetic  2.67 us (1%)
    unnamed x2, waiting for transfers between devices  63.8 us
    all_gather x1, blocking collectives, on_device(): lax.all_gather(attended, 'gx', axis=0, tiled=True)  30.6 us
    psum x1, blocking collectives, on_device(): lax.psum((jnp.sum(wide_in, axis=1), jnp.sum(wide_in * wide_in, axis=1)),...  23.1 us
    psum x1, blocking collectives, on_device(): branches = lax.psum(attn_part + mlp_part, 'gy')  10.5 us
    unnamed x35, local copies, waits for them, and re-layouts  8.57 us
    dot_general x1, matrix products, on_device(): up_partial = jnp.dot(mlp_in, w_up, preferred_element_type=jnp.float32)  4.61 us
    dot_general x1, matrix products, on_device(): mlp_part = jnp.dot(hidden, w_down, preferred_element_type=jnp.float32)  4.29 us
    dot_general x1, matrix products, on_device(): jnp.dot(attn_slot, w_qkv, preferred_element_type=jnp.float32)  4.1 us
  transfers between devices with their start and end apart: 1, of which 1 were waited for; matrix products, arithmetic and copies ran while one was open for 1% of the time, Pallas kernels for 0%

commit v1 on v0

v1 whole, which is shorter than its diff:
```python
import functools

import jax
import jax.numpy as jnp
import numpy as np
from jax import lax
from jax.experimental import pallas as pl
from jax.experimental.pallas import tpu as pltpu
from jax.sharding import PartitionSpec as P

HD = 128
ROT = 32
F32 = jnp.float32
BF16 = jnp.bfloat16
MESH = pl.DeviceIdType.MESH
ANY = pl.BlockSpec(memory_space=pl.ANY)
VMEM = pl.BlockSpec(memory_space=pltpu.VMEM)
SMEM = pl.BlockSpec(memory_space=pltpu.SMEM)


def slot_rows(asg_ref):
    requests = asg_ref.shape[1]
    slots = lax.broadcasted_iota(jnp.int32, (requests, requests), 0)
    return jnp.where(slots == asg_ref[...], 1.0, 0.0).astype(BF16)


def send(src, dst, ssem, rsem, where):
    copy = pltpu.make_async_remote_copy(
        src_ref=src, dst_ref=dst, send_sem=ssem, recv_sem=rsem,
        device_id=where, device_id_type=MESH,
    )
    copy.start()
    return copy


def project_kernel(
    n, m, h_ref, g1_ref, b1_ref, g2_ref, b2_ref, asg_ref, bq_ref, bu_ref, wq_hbm, wu_hbm,
    qkv_ref, hid_ref,
    wq, wu, st_own, st_in, q_send, q_in, u_part, u_send, u_in,
    wsem, s_ssem, s_rsem, q_ssem, q_rsem, u_ssem, u_rsem,
):
    me = lax.axis_index("gx")
    rg_count = n // m
    requests, depth = h_ref.shape
    rows = q_send.shape[1]
    u_rows, u_cols = u_send.shape[1:]
    my_col, my_group = lax.rem(me, m), me // m
    load_q = pltpu.make_async_copy(wq_hbm, wq, wsem.at[m])
    load_q.start()
    order = list(range(1, m)) + [0]
    loads = {}
    for k in order:
        col = lax.rem(my_col + k, m)
        loads[k] = pltpu.make_async_copy(
            wu_hbm.at[:, pl.ds(pl.multiple_of(col * u_cols, 128), u_cols)], wu.at[k], wsem.at[k]
        )
        loads[k].start()
    barrier = pltpu.get_barrier_semaphore()
    for k in range(1, n):
        pl.semaphore_signal(barrier, inc=1, device_id={"gx": lax.rem(me + k, n)}, device_id_type=MESH)

    place = slot_rows(asg_ref)
    x = jnp.dot(place, h_ref[...], preferred_element_type=F32)
    sums = jnp.sum(x, axis=1, keepdims=True)
    squares = jnp.sum(x * x, axis=1, keepdims=True)
    lane = lax.broadcasted_iota(jnp.int32, (requests, 128), 1)
    st_own[...] = jnp.where(lane == 0, sums, jnp.where(lane == 1, squares, 0.0))
    pl.semaphore_wait(barrier, n - 1)
    stats = [
        send(st_own, st_in.at[k], s_ssem.at[k], s_rsem.at[k], {"gx": lax.rem(me + k, n)})
        for k in range(1, n)
    ]
    total = st_own[...]
    for k in range(1, n):
        stats[k - 1].wait_recv()
        total = total + st_in[k]
    width = depth * n
    mean = total[:, 0:1] / width
    var = total[:, 1:2] / width - mean * mean
    normed = (x - mean) * lax.rsqrt(var + 1e-05)
    attn_in = (normed * g1_ref[...] + b1_ref[...]).astype(BF16)
    mlp_in = (normed * g2_ref[...] + b2_ref[...]).astype(BF16)

    load_q.wait()
    qkv = jnp.dot(attn_in, wq[...], preferred_element_type=F32)
    for p in range(n):
        q_send[p] = qkv[p * rows : (p + 1) * rows, :]
    q_copies = []
    for k in range(1, n):
        peer = lax.rem(me + k, n)
        q_copies.append(send(q_send.at[peer], q_in.at[k], q_ssem.at[k], q_rsem.at[k], {"gx": peer}))
    u_copies = []
    for k in order:
        loads[k].wait()
        part = jnp.dot(mlp_in, wu[k], preferred_element_type=F32)
        if rg_count > 1:
            u_part[...] = part
        for j in list(range(1, rg_count)) + [0]:
            group = lax.rem(my_group + j, rg_count)
            peer = group * m + lax.rem(my_col + k, m)
            at = j * m + k
            if rg_count > 1:
                own = u_part[pl.ds(pl.multiple_of(group * u_rows, u_rows), u_rows), :]
            else:
                own = part
            u_send[at] = own.astype(BF16)
            if at:
                u_copies.append(send(u_send.at[at], u_in.at[at], u_ssem.at[at], u_rsem.at[at], {"gx": peer}))
    total_q = q_send[me] + bq_ref[...]
    for k in range(1, n):
        q_copies[k - 1].wait_recv()
        total_q = total_q + q_in[k]
    qkv_ref[...] = total_q
    for copy in u_copies:
        copy.wait_recv()
    up = own.astype(F32) + bu_ref[my_col]
    for at in range(1, n):
        up = up + u_in[at].astype(F32)
    hid_ref[...] = (0.5 * up * (1.0 + lax.erf(up * np.float32(0.5**0.5)))).astype(BF16)
    for copy in stats + q_copies + u_copies:
        copy.wait_send()


def attend_kernel(
    len_ref, asg_ref, qkv_ref, freq_ref, k_hbm, v_hbm,
    att_ref, nk_hbm, nv_hbm,
    kbuf, vbuf, q_scr, k_scr, v_scr, sc, o_scr, isem, osem,
):
    rows, heads, span, _ = kbuf.shape
    requests = len_ref.shape[0]
    first = lax.axis_index("gx") * rows
    loads = []
    for s in range(rows):
        for i, (hbm, buf) in enumerate(((k_hbm, kbuf), (v_hbm, vbuf))):
            copy = pltpu.make_async_copy(hbm.at[s], buf.at[s], isem.at[2 * s + i])
            copy.start()
            loads.append(copy)
    lane = lax.broadcasted_iota(jnp.int32, (1, HD), 1)
    half = ROT // 2
    places = lax.broadcasted_iota(jnp.int32, (heads, span), 1)
    stores = []
    for s in range(rows):
        def find(r, value):
            return jnp.where(asg_ref[r] == first + s, len_ref[r], value)
        length = lax.fori_loop(0, requests, find, jnp.int32(1))
        position = length - 1
        angle = position.astype(F32) * freq_ref[...]
        cosine, sine = jnp.cos(angle), jnp.sin(angle)
        c = jnp.where(lane < ROT, cosine, 1.0)
        s1 = jnp.where(lane < half, -sine, 0.0)
        s2 = jnp.where((lane >= half) & (lane < ROT), sine, 0.0)

        def turn(t):
            return t * c + pltpu.roll(t, HD - half, 1) * s1 + pltpu.roll(t, half, 1) * s2

        for h in range(heads):
            q_scr[h : h + 1, :] = qkv_ref[s : s + 1, (3 * h) * HD : (3 * h + 1) * HD]
            k_scr[h : h + 1, :] = qkv_ref[s : s + 1, (3 * h + 1) * HD : (3 * h + 2) * HD]
            v_scr[h : h + 1, :] = qkv_ref[s : s + 1, (3 * h + 2) * HD : (3 * h + 3) * HD]
        query = turn(q_scr[...]).astype(BF16)
        new_key = turn(k_scr[...])
        new_value = v_scr[...]
        base = pl.multiple_of((position // 16) * 16, 16)
        hit = lax.broadcasted_iota(jnp.int32, (16, HD), 0) == position - base
        for i, (buf, hbm, fresh) in enumerate(((kbuf, nk_hbm, new_key), (vbuf, nv_hbm, new_value))):
            loads[2 * s + i].wait()
            for h in range(heads):
                old = buf[s, h, pl.ds(base, 16), :].astype(F32)
                buf[s, h, pl.ds(base, 16), :] = jnp.where(hit, fresh[h : h + 1, :], old).astype(BF16)
            copy = pltpu.make_async_copy(buf.at[s], hbm.at[s], osem.at[2 * s + i])
            copy.start()
            stores.append(copy)
            if i == 0:
                for h in range(heads):
                    sc[h : h + 1, :] = lax.dot_general(
                        query[h : h + 1, :], kbuf[s, h], (((1,), (1,)), ((), ())),
                        preferred_element_type=F32,
                    )
                scores = sc[0:heads, :] * np.float32(HD**-0.5)
                valid = places < length
                scores = jnp.where(valid, scores, -1e30)
                top = jnp.max(scores, axis=1, keepdims=True)
                weights = jnp.where(valid, jnp.exp(scores - top), 0.0)
                total = jnp.sum(weights, axis=1, keepdims=True)
                low = weights.astype(BF16)
        for h in range(heads):
            o_scr[h : h + 1, :] = jnp.dot(low[h : h + 1, :], vbuf[s, h], preferred_element_type=F32)
        out = (o_scr[0:heads, :] / total).astype(BF16).astype(F32)
        for h in range(heads):
            att_ref[s : s + 1, h * HD : (h + 1) * HD] = out[h : h + 1, :]
    for copy in stores:
        copy.wait()


def output_kernel(
    n, m, ny, att_ref, hid_ref, h_ref, asg_ref, bo_ref, bd_ref, wo_hbm, wd_hbm,
    out_ref,
    wo, wd, h_all, a_all, a_rows, y_send, y_in,
    wsem, h_ssem, h_rsem, a_ssem, a_rsem, y_ssem, y_rsem,
):
    me, my = lax.axis_index("gx"), lax.axis_index("gy")
    rows = att_ref.shape[0]
    cols = hid_ref.shape[1]
    load_d = pltpu.make_async_copy(wd_hbm, wd, wsem.at[0])
    load_o = pltpu.make_async_copy(wo_hbm, wo, wsem.at[1])
    load_d.start()
    load_o.start()
    barrier = pltpu.get_barrier_semaphore()
    for k in range(1, n):
        pl.semaphore_signal(barrier, inc=1, device_id={"gx": lax.rem(me + k, n)}, device_id_type=MESH)
    for k in range(1, ny):
        pl.semaphore_signal(barrier, inc=1, device_id={"gy": lax.rem(my + k, ny)}, device_id_type=MESH)
    h_all[me] = hid_ref[...]
    a_all[me] = att_ref[...]
    pl.semaphore_wait(barrier, n + ny - 2)
    a_copies, h_copies = [], []
    for k in range(1, n):
        peer = {"gx": lax.rem(me + k, n)}
        h_copies.append(send(h_all.at[me], h_all.at[me], h_ssem.at[k], h_rsem.at[k], peer))
    for k in range(1, n):
        peer = {"gx": lax.rem(me + k, n)}
        a_copies.append(send(a_all.at[me], a_all.at[me], a_ssem.at[k], a_rsem.at[k], peer))
    place = slot_rows(asg_ref)
    x = jnp.dot(place, h_ref[...], preferred_element_type=F32) + bo_ref[...] + bd_ref[...]
    for copy in h_copies:
        copy.wait_recv()
    load_d.wait()
    acc = jnp.zeros(y_send.shape, F32)
    for c in range(m):
        parts = [h_all[g * m + c] for g in range(n // m)]
        block = parts[0] if len(parts) == 1 else jnp.concatenate(parts, axis=0)
        acc = acc + jnp.dot(block, wd[c * cols : (c + 1) * cols, :], preferred_element_type=F32)
    for copy in a_copies:
        copy.wait_recv()
    for p in range(n):
        a_rows[p * rows : (p + 1) * rows, :] = a_all[p]
    load_o.wait()
    acc = acc + jnp.dot(a_rows[...].astype(BF16), wo[...], preferred_element_type=F32)
    y_send[...] = acc
    y_copies = []
    for k in range(1, ny):
        peer = {"gy": lax.rem(my + k, ny)}
        y_copies.append(send(y_send, y_in.at[k], y_ssem.at[k], y_rsem.at[k], peer))
    acc = acc + x
    for k in range(1, ny):
        y_copies[k - 1].wait_recv()
        acc = acc + y_in[k]
    out_ref[...] = lax.dot_general(
        place, acc.astype(BF16), (((0,), (0,)), ((), ())), preferred_element_type=F32
    ).astype(BF16)
    for copy in h_copies + a_copies + y_copies:
        copy.wait_send()


def on_device(
    n, ny, hidden_in, norm1_gain, norm1_bias, norm2_gain, norm2_bias, w_qkv, b_qkv, w_out, b_out,
    w_up, b_up, w_down, b_down, key_cache, value_cache, lengths, assignment,
):
    requests, depth = hidden_in.shape
    rows, heads, span, _ = key_cache.shape
    q_cols = w_qkv.shape[1]
    units = w_up.shape[1]
    m = max(c for c in range(1, n + 1) if n % c == 0 and units % c == 0 and (units // c) % 128 == 0)
    u_rows, u_cols = requests // (n // m), units // m
    asg = assignment.reshape(1, requests)
    dma = pltpu.SemaphoreType.DMA
    row = lambda a: a.reshape(1, a.shape[0])

    qkv, hid = pl.pallas_call(
        functools.partial(project_kernel, n, m),
        out_shape=(
            jax.ShapeDtypeStruct((rows, q_cols), F32),
            jax.ShapeDtypeStruct((u_rows, u_cols), BF16),
        ),
        in_specs=[VMEM] * 8 + [ANY] * 2,
        out_specs=(VMEM, VMEM),
        scratch_shapes=[
            pltpu.VMEM((depth, q_cols), BF16),
            pltpu.VMEM((m, depth, u_cols), BF16),
            pltpu.VMEM((requests, 128), F32),
            pltpu.VMEM((n, requests, 128), F32),
            pltpu.VMEM((n, rows, q_cols), F32),
            pltpu.VMEM((n, rows, q_cols), F32),
            pltpu.VMEM((requests, u_cols), F32),
            pltpu.VMEM((n, u_rows, u_cols), BF16),
            pltpu.VMEM((n, u_rows, u_cols), BF16),
            dma((m + 1,)),
            dma((n,)), dma((n,)), dma((n,)), dma((n,)), dma((n,)), dma((n,)),
        ],
        compiler_params=pltpu.CompilerParams(
            collective_id=0, has_side_effects=True, vmem_limit_bytes=24 << 20
        ),
        name="project",
    )(
        hidden_in, row(norm1_gain), row(norm1_bias), row(norm2_gain), row(norm2_bias), asg,
        row(b_qkv), b_up.reshape(m, 1, u_cols), w_qkv, w_up,
    )

    freq = np.zeros((1, HD), np.float32)
    freq[0, :ROT] = np.tile(10000.0 ** (-2.0 * np.arange(ROT // 2) / ROT), 2)
    padded = -(-heads // 8) * 8
    att, new_keys, new_values = pl.pallas_call(
        attend_kernel,
        out_shape=(
            jax.ShapeDtypeStruct((rows, heads * HD), F32),
            jax.ShapeDtypeStruct(key_cache.shape, BF16),
            jax.ShapeDtypeStruct(value_cache.shape, BF16),
        ),
        in_specs=[SMEM, SMEM, VMEM, VMEM, ANY, ANY],
        out_specs=(VMEM, ANY, ANY),
        scratch_shapes=[
            pltpu.VMEM((rows, heads, span, HD), BF16),
            pltpu.VMEM((rows, heads, span, HD), BF16),
            pltpu.VMEM((padded, HD), F32),
            pltpu.VMEM((padded, HD), F32),
            pltpu.VMEM((padded, HD), F32),
            pltpu.VMEM((padded, span), F32),
            pltpu.VMEM((padded, HD), F32),
            dma((2 * rows,)),
            dma((2 * rows,)),
        ],
        compiler_params=pltpu.CompilerParams(vmem_limit_bytes=20 << 20),
        name="attend",
    )(lengths, assignment, qkv, jnp.asarray(freq), key_cache, value_cache)

    hidden_out = pl.pallas_call(
        functools.partial(output_kernel, n, m, ny),
        out_shape=jax.ShapeDtypeStruct((requests, depth), BF16),
        in_specs=[VMEM] * 6 + [ANY] * 2,
        out_specs=VMEM,
        scratch_shapes=[
            pltpu.VMEM(w_out.shape, BF16),
            pltpu.VMEM(w_down.shape, BF16),
            pltpu.VMEM((n, u_rows, u_cols), BF16),
            pltpu.VMEM((n, rows, heads * HD), F32),
            pltpu.VMEM((requests, heads * HD), F32),
            pltpu.VMEM((requests, depth), F32),
            pltpu.VMEM((ny, requests, depth), F32),
            dma((2,)),
            dma((n,)), dma((n,)), dma((n,)), dma((n,)), dma((ny,)), dma((ny,)),
        ],
        compiler_params=pltpu.CompilerParams(
            collective_id=1, has_side_effects=True, vmem_limit_bytes=20 << 20
        ),
        name="output",
    )(att, hid, hidden_in, asg, row(b_out), row(b_down), w_out, w_down)
    return (hidden_out, new_keys, new_values)


def solution(mesh):
    return jax.shard_map(
        functools.partial(on_device, mesh.shape["gx"], mesh.shape["gy"]),
        mesh=mesh,
        in_specs=(
            P(None, "gx"), P("gx"), P("gx"), P("gx"), P("gx"),
            P("gx", "gy"), P("gy"), P("gy", "gx"), P("gx"),
            P("gx", "gy"), P("gy"), P("gy", "gx"), P("gx"),
            P("gx", "gy", None, None), P("gx", "gy", None, None), P(), P(),
        ),
        out_specs=(P(None, "gx"), P("gx", "gy", None, None), P("gx", "gy", None, None)),
        check_vma=False,
    )
```

time: 186 us -> 54.4 us (0.29)
  blocking collectives: 64.2 us -> 0 us
  waiting for transfers between devices: 63.8 us -> 0 us
  Pallas kernels: 0 us -> 41.6 us
  matrix products: 20.7 us -> 0 us
  between operations: 18.9 us -> 0.78 us
  local copies, waits for them, and re-layouts: 15 us -> 11.5 us
  other arithmetic: 2.67 us -> 0 us
    unnamed x2 -> x0, waiting for transfers between devices: 63.8 us -> none
    pallas_call x0 -> x3, Pallas kernels: none -> 41.6 us  [the longest x1 22.5 us: on_device(): pl.pallas_call(functools.partial(project_kernel, n, m), out_shape=(jax.Sh...]
    psum x2 -> x0, blocking collectives: 33.6 us -> none  [the longest x1 23.1 us: on_device(): lax.psum((jnp.sum(wide_in, axis=1), jnp.sum(wide_in * wide_in, axis=1)),...]
    all_gather x1 -> x0, blocking collectives: 30.6 us -> none  [on_device(): lax.all_gather(attended, 'gx', axis=0, tiled=True)]
    dot_general x7 -> x0, matrix products: 20.7 us -> none  [the longest x1 4.61 us: on_device(): up_partial = jnp.dot(mlp_in, w_up, preferred_element_type=jnp.float32)]
    dynamic_update_slice x4 -> x0, local copies, waits for them, and re-layouts: 5.44 us -> none  [the longest x2 2.73 us: on_device(): lax.dynamic_update_slice(new_keys, new_key[local_slot][None, :, None, :],...]
    reshape x1 -> x7, local copies, waits for them, and re-layouts: 0.03 us -> 3.49 us  [on_device(): row = lambda a: a.reshape(1, a.shape[0])]
    unnamed x35 -> x27, local copies, waits for them, and re-layouts: 8.57 us -> 8.01 us
  transfers between devices with their start and end apart: 1 -> 0, of which waited for: 1 -> 0; matrix products, arithmetic and copies ran while one was open for 1% -> 0% of each run, Pallas kernels for 0% -> 0%
where the time goes in v1:
time: 54.4 us; the launch traced here: 53.9 us
  Pallas kernels  41.6 us (76%)
  local copies, waits for them, and re-layouts  11.5 us (21%)
  between operations  0.78 us (1%)
    pallas_call x1, Pallas kernels, on_device(): pl.pallas_call(functools.partial(project_kernel, n, m), out_shape=(jax.Sh...  22.5 us
    pallas_call x1, Pallas kernels, on_device(): pl.pallas_call(functools.partial(output_kernel, n, m, ny), out_shape=jax....  12.9 us
    unnamed x27, local copies, waits for them, and re-layouts  8.01 us
    pallas_call x1, Pallas kernels, on_device(): pl.pallas_call(attend_kernel, out_shape=(jax.ShapeDtypeStruct((rows, head...  6.25 us
    reshape x7, local copies, waits for them, and re-layouts, on_device(): row = lambda a: a.reshape(1, a.shape[0])  3.49 us

profile of v1, /device:TPU:0, one launch (start us, length us, event | category | flops | bytes accessed | tf_op | source)
XLA Modules:
  0.0 53.9 jit_solution(4395601079041687308)
XLA Ops:
  0.6 0.7 %reshape.38.bq_ref = f32[1,3840]{1,0:T(1,128)S(1)} reshape(f32[3840]{0:T(1024)} %param.24) | data formatting | bytes 30720 | tf_op jit(solution)/shard_map/reshape | solution.py:267
  1.4 0.7 %reshape.33.g1_ref = f32[1,640]{1,0:T(1,128)S(1)} reshape(f32[640]{0:T(1024)} %param.19) | data formatting | bytes 5120 | tf_op jit(solution)/shard_map/reshape | solution.py:267
  2.1 0.7 %reshape.34.b1_ref = f32[1,640]{1,0:T(1,128)S(1)} reshape(f32[640]{0:T(1024)} %param.20) | data formatting | bytes 5120 | tf_op jit(solution)/shard_map/reshape | solution.py:267
  2.7 0.7 %reshape.35.g2_ref = f32[1,640]{1,0:T(1,128)S(1)} reshape(f32[640]{0:T(1024)} %param.21) | data formatting | bytes 5120 | tf_op jit(solution)/shard_map/reshape | solution.py:267
  3.4 0.7 %reshape.36.b2_ref = f32[1,640]{1,0:T(1,128)S(1)} reshape(f32[640]{0:T(1024)} %param.22) | data formatting | bytes 5120 | tf_op jit(solution)/shard_map/reshape | solution.py:267
  4.1 0.0 copy-start
  4.1 2.9 %copy-done = bf16[640,5120]{1,0:T(8,128)(2,1)S(1)} copy-done((bf16[640,5120]{1,0:T(8,128)(2,1)S(1)}, bf16[640,5120]{1,0:T(8,128)(2,1)}, u32[]{:S(2)}) %copy-start) | copy-done | bytes 6553624
  7.0 0.0 copy-start.4
  7.0 2.4 %copy-done.4 = bf16[640,3840]{1,0:T(8,128)(2,1)S(1)} copy-done((bf16[640,3840]{1,0:T(8,128)(2,1)S(1)}, bf16[640,3840]{1,0:T(8,128)(2,1)}, u32[]{:S(2)}) %copy-start.4) | copy-done | bytes 4915224
  9.4 0.0 copy-start.6
  9.4 0.7 %copy-done.6 = bf16[16,640]{1,0:T(8,128)(2,1)S(1)} copy-done((bf16[16,640]{1,0:T(8,128)(2,1)S(1)}, bf16[16,640]{1,0:T(8,128)(2,1)}, u32[]{:S(2)}) %copy-start.6) | copy-done | bytes 20504
  10.1 0.0 copy-start.7
  10.1 0.7 %copy-done.7 = f32[5120]{0:T(1024)S(1)} copy-done((f32[5120]{0:T(1024)S(1)}, f32[5120]{0:T(1024)}, u32[]{:S(2)}) %copy-start.7) | copy-done | bytes 20504
  10.8 0.0 copy-start.8
  10.8 0.7 %copy-done.8 = s32[16]{0:T(128)S(1)} copy-done((s32[16]{0:T(128)S(1)}, s32[16]{0:T(128)}, u32[]{:S(2)}) %copy-start.8) | copy-done | bytes 88
  11.5 0.0 copy-start.2
  11.5 0.0 copy-start.3
  11.5 0.0 copy-start.9
  11.5 0.0 copy-start.10
  11.5 22.5 %project.1 = (f32[2,3840]{1,0:T(2,128)S(1)}, bf16[16,640]{1,0:T(8,128)(2,1)S(1)}) custom-call(bf16[16,640]{1,0:T(8,128)(2,1)S(1)} %copy-done.6, f32[1,640]{1,0:T(1,128)S(1)} %reshape.33.g1_ref, f32[1,640]{1,0:T(1,128)S(1)} %reshape.34.b1_ref, f32[1,640]{1,0:T(1,128)S(1)} %reshape.35.g2_ref, f32[1,640]{1,0:T(1,128)S(1)} %reshape.36.b2_ref, ...), custom_call_target="tpu_custom_call" | custom-call | tf_op jit(solution)/shard_map/project/pallas_call | solution.py:269
  34.0 0.0 copy-done.2
  34.0 0.0 copy-done.3
  34.0 0.0 copy-done.9
  34.0 0.0 copy-done.10
  34.0 0.0 copy-start.11
  34.0 0.0 copy-start.12
  34.0 0.0 copy-start.1
  34.0 0.0 copy-start.5
  34.0 6.2 %attend.1 = (f32[2,1280]{1,0:T(2,128)S(1)}, bf16[2,10,1024,128]{3,2,1,0:T(8,128)(2,1)}, bf16[2,10,1024,128]{3,2,1,0:T(8,128)(2,1)}) custom-call(s32[16]{0:T(128)S(1)} %copy-done.9, s32[16]{0:T(128)S(1)} %copy-done.8, f32[2,3840]{1,0:T(2,128)S(1)} %get-tuple-element.8.qkv_ref, f32[1,128]{1,0:T(1,128)S(1)} %copy-done.10, ...), custom_call_target="tpu_custom_call" | custom-call | tf_op jit(solution)/shard_map/attend/pallas_call | solution.py:302
  40.3 0.0 copy-done.11
  40.3 0.0 copy-done.12
  40.3 0.0 copy-done.1
  40.4 0.0 copy-done.5
  40.4 12.9 %output.1 = bf16[16,640]{1,0:T(8,128)(2,1)S(1)} custom-call(f32[2,1280]{1,0:T(2,128)S(1)} %get-tuple-element.9.att_ref, bf16[16,640]{1,0:T(8,128)(2,1)S(1)} %get-tuple-element.10.hid_ref, bf16[16,640]{1,0:T(8,128)(2,1)S(1)} %copy-done.6, s32[1,16]{1,0:T(1,128)S(1)} %bitcast.4, f32[1,640]{1,0:T(1,128)S(1)} %reshape.40.bo_ref, f32[1,640]{1,0:T(1,128)S(1)} %reshape.41.bd_ref, ...), custom_call_target="tpu_custom_call" | custom-call | tf_op jit(solution)/shard_map/output/pallas_call | solution.py:326
  53.3 0.6 %copy.22 = bf16[16,640]{1,0:T(8,128)(2,1)} copy(bf16[16,640]{1,0:T(8,128)(2,1)S(1)} %output.1) | data formatting | bytes 40960
  (2 shorter events, 0.0 us)
Async XLA Ops:
  4.1 2.9 %copy-start = (bf16[640,5120]{1,0:T(8,128)(2,1)S(1)}, bf16[640,5120]{1,0:T(8,128)(2,1)}, u32[]{:S(2)}) copy-start(bf16[640,5120]{1,0:T(8,128)(2,1)} %wu_hbm.1) | copy-start | bytes 19660804
  7.0 2.4 %copy-start.4 = (bf16[640,3840]{1,0:T(8,128)(2,1)S(1)}, bf16[640,3840]{1,0:T(8,128)(2,1)}, u32[]{:S(2)}) copy-start(bf16[640,3840]{1,0:T(8,128)(2,1)} %wq_hbm.1) | copy-start | bytes 14745604
  9.4 0.7 %copy-start.6 = (bf16[16,640]{1,0:T(8,128)(2,1)S(1)}, bf16[16,640]{1,0:T(8,128)(2,1)}, u32[]{:S(2)}) copy-start(bf16[16,640]{1,0:T(8,128)(2,1)} %h_ref.3) | copy-start | bytes 61444
  10.1 0.7 %copy-start.7 = (f32[5120]{0:T(1024)S(1)}, f32[5120]{0:T(1024)}, u32[]{:S(2)}) copy-start(f32[5120]{0:T(1024)} %param.28) | copy-start | bytes 61444
  10.8 0.7 %copy-start.8 = (s32[16]{0:T(128)S(1)}, s32[16]{0:T(128)}, u32[]{:S(2)}) copy-start(s32[16]{0:T(128)} %asg_ref.1) | copy-start | bytes 196
  11.5 22.5 %copy-start.2 = (bf16[2,10,1024,128]{3,2,1,0:T(8,128)(2,1)S(1)}, bf16[2,10,1024,128]{3,2,1,0:T(8,128)(2,1)}, u32[]{:S(2)}) copy-start(bf16[2,10,1024,128]{3,2,1,0:T(8,128)(2,1)} %k_hbm.1) | copy-start | bytes 15728644
  11.5 22.5 %copy-start.3 = (bf16[2,10,1024,128]{3,2,1,0:T(8,128)(2,1)S(1)}, bf16[2,10,1024,128]{3,2,1,0:T(8,128)(2,1)}, u32[]{:S(2)}) copy-start(bf16[2,10,1024,128]{3,2,1,0:T(8,128)(2,1)} %v_hbm.1) | copy-start | bytes 15728644
  11.5 22.5 %copy-start.9 = (s32[16]{0:T(128)S(1)}, s32[16]{0:T(128)}, u32[]{:S(2)}) copy-start(s32[16]{0:T(128)} %len_ref.1) | copy-start | bytes 196
  11.5 22.5 %copy-start.10 = (f32[1,128]{1,0:T(1,128)S(1)}, f32[1,128]{1,0:T(1,128)}, u32[]{:S(2)}) copy-start(f32[1,128]{1,0:T(1,128)} %constant.2.clone.freq_ref) | copy-start | bytes 1540
  34.0 6.3 %copy-start.11 = (f32[640]{0:T(1024)S(1)}, f32[640]{0:T(1024)}, u32[]{:S(2)}) copy-start(f32[640]{0:T(1024)} %param.26) | copy-start | bytes 7684
  34.0 6.3 %copy-start.12 = (f32[640]{0:T(1024)S(1)}, f32[640]{0:T(1024)}, u32[]{:S(2)}) copy-start(f32[640]{0:T(1024)} %param.30) | copy-start | bytes 7684
  34.0 6.3 %copy-start.1 = (bf16[5120,640]{1,0:T(8,128)(2,1)S(1)}, bf16[5120,640]{1,0:T(8,128)(2,1)}, u32[]{:S(2)}) copy-start(bf16[5120,640]{1,0:T(8,128)(2,1)} %wd_hbm.1) | copy-start | bytes 19660804
  34.0 6.3 %copy-start.5 = (bf16[1280,640]{1,0:T(8,128)(2,1)S(1)}, bf16[1280,640]{1,0:T(8,128)(2,1)}, u32[]{:S(2)}) copy-start(bf16[1280,640]{1,0:T(8,128)(2,1)} %wo_hbm.1) | copy-start | bytes 4915204

commit v2 on v1

--- a/solution.py
+++ b/solution.py
@@ -16,6 +16,7 @@
 ANY = pl.BlockSpec(memory_space=pl.ANY)
 VMEM = pl.BlockSpec(memory_space=pltpu.VMEM)
 SMEM = pl.BlockSpec(memory_space=pltpu.SMEM)
+HBM = pl.BlockSpec(memory_space=pltpu.HBM)
 
 
 def slot_rows(asg_ref):
@@ -34,15 +35,16 @@
 
 
 def project_kernel(
-    n, m, h_ref, g1_ref, b1_ref, g2_ref, b2_ref, asg_ref, bq_ref, bu_ref, wq_hbm, wu_hbm,
+    n, m, h_ref, g1_ref, b1_ref, g2_ref, b2_ref, asg_ref, bu_ref, wq_hbm, wu_hbm,
     qkv_ref, hid_ref,
-    wq, wu, st_own, st_in, q_send, q_in, u_part, u_send, u_in,
+    wq, wu, st_own, st_in, q_wide, q_send, q_in, u_part, u_send, u_in,
     wsem, s_ssem, s_rsem, q_ssem, q_rsem, u_ssem, u_rsem,
 ):
     me = lax.axis_index("gx")
     rg_count = n // m
     requests, depth = h_ref.shape
-    rows = q_send.shape[1]
+    rows = requests // n
+    tiles = wq.shape[1] // HD
     u_rows, u_cols = u_send.shape[1:]
     my_col, my_group = lax.rem(me, m), me // m
     load_q = pltpu.make_async_copy(wq_hbm, wq, wsem.at[m])
@@ -78,13 +80,17 @@
     mean = total[:, 0:1] / width
     var = total[:, 1:2] / width - mean * mean
     normed = (x - mean) * lax.rsqrt(var + 1e-05)
-    attn_in = (normed * g1_ref[...] + b1_ref[...]).astype(BF16)
-    mlp_in = (normed * g2_ref[...] + b2_ref[...]).astype(BF16)
+    attn_in = (normed * g1_ref[...].reshape(1, depth) + b1_ref[...].reshape(1, depth)).astype(BF16)
+    mlp_in = (normed * g2_ref[...].reshape(1, depth) + b2_ref[...].reshape(1, depth)).astype(BF16)
 
     load_q.wait()
     qkv = jnp.dot(attn_in, wq[...], preferred_element_type=F32)
     for p in range(n):
-        q_send[p] = qkv[p * rows : (p + 1) * rows, :]
+        for j in range(tiles):
+            q_wide[p, j * rows : (j + 1) * rows, :] = qkv[
+                p * rows : (p + 1) * rows, j * HD : (j + 1) * HD
+            ]
+    q_send[...] = q_wide[...].astype(BF16)
     q_copies = []
     for k in range(1, n):
         peer = lax.rem(me + k, n)
@@ -106,10 +112,10 @@
             u_send[at] = own.astype(BF16)
             if at:
                 u_copies.append(send(u_send.at[at], u_in.at[at], u_ssem.at[at], u_rsem.at[at], {"gx": peer}))
-    total_q = q_send[me] + bq_ref[...]
+    total_q = q_wide[me]
     for k in range(1, n):
         q_copies[k - 1].wait_recv()
-        total_q = total_q + q_in[k]
+        total_q = total_q + q_in[k].astype(F32)
     qkv_ref[...] = total_q
     for copy in u_copies:
         copy.wait_recv()
@@ -122,23 +128,23 @@
 
 
 def attend_kernel(
-    len_ref, asg_ref, qkv_ref, freq_ref, k_hbm, v_hbm,
+    len_ref, asg_ref, qkv_ref, bq_ref, freq_ref, kbuf, vbuf,
     att_ref, nk_hbm, nv_hbm,
-    kbuf, vbuf, q_scr, k_scr, v_scr, sc, o_scr, isem, osem,
+    q_scr, k_scr, v_scr, sc, o_scr, group, osem, gsem,
 ):
     rows, heads, span, _ = kbuf.shape
     requests = len_ref.shape[0]
     first = lax.axis_index("gx") * rows
-    loads = []
-    for s in range(rows):
-        for i, (hbm, buf) in enumerate(((k_hbm, kbuf), (v_hbm, vbuf))):
-            copy = pltpu.make_async_copy(hbm.at[s], buf.at[s], isem.at[2 * s + i])
+    whole = []
+    for i, (buf, hbm) in enumerate(((kbuf, nk_hbm), (vbuf, nv_hbm))):
+        for s in range(rows):
+            copy = pltpu.make_async_copy(buf.at[s], hbm.at[s], osem.at[2 * s + i])
             copy.start()
-            loads.append(copy)
+            whole.append((s, i, copy))
     lane = lax.broadcasted_iota(jnp.int32, (1, HD), 1)
     half = ROT // 2
     places = lax.broadcasted_iota(jnp.int32, (heads, span), 1)
-    stores = []
+    bases = []
     for s in range(rows):
         def find(r, value):
             return jnp.where(asg_ref[r] == first + s, len_ref[r], value)
@@ -154,57 +160,62 @@
             return t * c + pltpu.roll(t, HD - half, 1) * s1 + pltpu.roll(t, half, 1) * s2
 
         for h in range(heads):
-            q_scr[h : h + 1, :] = qkv_ref[s : s + 1, (3 * h) * HD : (3 * h + 1) * HD]
-            k_scr[h : h + 1, :] = qkv_ref[s : s + 1, (3 * h + 1) * HD : (3 * h + 2) * HD]
-            v_scr[h : h + 1, :] = qkv_ref[s : s + 1, (3 * h + 2) * HD : (3 * h + 3) * HD]
-        query = turn(q_scr[...]).astype(BF16)
-        new_key = turn(k_scr[...])
-        new_value = v_scr[...]
+            for i, scr in enumerate((q_scr, k_scr, v_scr)):
+                j = 3 * h + i
+                at = j * rows + s
+                scr[h : h + 1, :] = qkv_ref[at : at + 1, :] + bq_ref[j : j + 1, :]
+        query = turn(q_scr[0:heads, :]).astype(BF16)
+        new_key = turn(k_scr[0:heads, :]).astype(BF16).astype(F32)
+        new_value = v_scr[0:heads, :].astype(BF16).astype(F32)
         base = pl.multiple_of((position // 16) * 16, 16)
+        bases.append(base)
         hit = lax.broadcasted_iota(jnp.int32, (16, HD), 0) == position - base
-        for i, (buf, hbm, fresh) in enumerate(((kbuf, nk_hbm, new_key), (vbuf, nv_hbm, new_value))):
-            loads[2 * s + i].wait()
+        for i, (buf, fresh) in enumerate(((kbuf, new_key), (vbuf, new_value))):
             for h in range(heads):
                 old = buf[s, h, pl.ds(base, 16), :].astype(F32)
-                buf[s, h, pl.ds(base, 16), :] = jnp.where(hit, fresh[h : h + 1, :], old).astype(BF16)
-            copy = pltpu.make_async_copy(buf.at[s], hbm.at[s], osem.at[2 * s + i])
-            copy.start()
-            stores.append(copy)
-            if i == 0:
-                for h in range(heads):
-                    sc[h : h + 1, :] = lax.dot_general(
-                        query[h : h + 1, :], kbuf[s, h], (((1,), (1,)), ((), ())),
-                        preferred_element_type=F32,
-                    )
-                scores = sc[0:heads, :] * np.float32(HD**-0.5)
-                valid = places < length
-                scores = jnp.where(valid, scores, -1e30)
-                top = jnp.max(scores, axis=1, keepdims=True)
-                weights = jnp.where(valid, jnp.exp(scores - top), 0.0)
-                total = jnp.sum(weights, axis=1, keepdims=True)
-                low = weights.astype(BF16)
+                group[i, s, h] = jnp.where(hit, fresh[h : h + 1, :], old).astype(BF16)
+        for h in range(heads):
+            sc[h : h + 1, :] = lax.dot_general(
+                query[h : h + 1, :], kbuf[s, h], (((1,), (1,)), ((), ())),
+                preferred_element_type=F32,
+            )
+        scale = np.float32(HD**-0.5)
+        fresh_score = jnp.sum(query.astype(F32) * new_key, axis=1, keepdims=True) * scale
+        scores = jnp.where(places < position, sc[0:heads, :] * scale, -1e30)
+        top = jnp.maximum(jnp.max(scores, axis=1, keepdims=True), fresh_score)
+        weights = jnp.where(places < position, jnp.exp(scores - top), 0.0)
+        fresh_weight = jnp.exp(fresh_score - top)
+        total = jnp.sum(weights, axis=1, keepdims=True) + fresh_weight
+        low = weights.astype(BF16)
         for h in range(heads):
             o_scr[h : h + 1, :] = jnp.dot(low[h : h + 1, :], vbuf[s, h], preferred_element_type=F32)
-        out = (o_scr[0:heads, :] / total).astype(BF16).astype(F32)
+        summed = o_scr[0:heads, :] + fresh_weight.astype(BF16).astype(F32) * new_value
+        out = (summed / total).astype(BF16).astype(F32)
         for h in range(heads):
             att_ref[s : s + 1, h * HD : (h + 1) * HD] = out[h : h + 1, :]
-    for copy in stores:
+    parts = []
+    for s, i, copy in whole:
         copy.wait()
+        part = pltpu.make_async_copy(
+            group.at[i, s],
+            (nk_hbm, nv_hbm)[i].at[s, :, pl.ds(bases[s], 16), :],
+            gsem.at[2 * s + i],
+        )
+        part.start()
+        parts.append(part)
+    for part in parts:
+        part.wait()
 
 
 def output_kernel(
-    n, m, ny, att_ref, hid_ref, h_ref, asg_ref, bo_ref, bd_ref, wo_hbm, wd_hbm,
+    n, m, ny, att_ref, hid_ref, h_ref, asg_ref, bo_ref, bd_ref, wo, wd,
     out_ref,
-    wo, wd, h_all, a_all, a_rows, y_send, y_in,
-    wsem, h_ssem, h_rsem, a_ssem, a_rsem, y_ssem, y_rsem,
+    h_all, a_all, a_rows, y_send, y_in,
+    h_ssem, h_rsem, a_ssem, a_rsem, y_ssem, y_rsem,
 ):
     me, my = lax.axis_index("gx"), lax.axis_index("gy")
     rows = att_ref.shape[0]
     cols = hid_ref.shape[1]
-    load_d = pltpu.make_async_copy(wd_hbm, wd, wsem.at[0])
-    load_o = pltpu.make_async_copy(wo_hbm, wo, wsem.at[1])
-    load_d.start()
-    load_o.start()
     barrier = pltpu.get_barrier_semaphore()
     for k in range(1, n):
         pl.semaphore_signal(barrier, inc=1, device_id={"gx": lax.rem(me + k, n)}, device_id_type=MESH)
@@ -221,10 +232,9 @@
         peer = {"gx": lax.rem(me + k, n)}
         a_copies.append(send(a_all.at[me], a_all.at[me], a_ssem.at[k], a_rsem.at[k], peer))
     place = slot_rows(asg_ref)
-    x = jnp.dot(place, h_ref[...], preferred_element_type=F32) + bo_ref[...] + bd_ref[...]
+    x = jnp.dot(place, h_ref[...], preferred_element_type=F32) + (bo_ref[...] + bd_ref[...]).reshape(1, h_ref.shape[1])
     for copy in h_copies:
         copy.wait_recv()
-    load_d.wait()
     acc = jnp.zeros(y_send.shape, F32)
     for c in range(m):
         parts = [h_all[g * m + c] for g in range(n // m)]
@@ -234,9 +244,8 @@
         copy.wait_recv()
     for p in range(n):
         a_rows[p * rows : (p + 1) * rows, :] = a_all[p]
-    load_o.wait()
     acc = acc + jnp.dot(a_rows[...].astype(BF16), wo[...], preferred_element_type=F32)
-    y_send[...] = acc
+    y_send[...] = acc.astype(BF16)
     y_copies = []
     for k in range(1, ny):
         peer = {"gy": lax.rem(my + k, ny)}
@@ -244,7 +253,7 @@
     acc = acc + x
     for k in range(1, ny):
         y_copies[k - 1].wait_recv()
-        acc = acc + y_in[k]
+        acc = acc + y_in[k].astype(F32)
     out_ref[...] = lax.dot_general(
         place, acc.astype(BF16), (((0,), (0,)), ((), ())), preferred_element_type=F32
     ).astype(BF16)
@@ -264,23 +273,24 @@
     u_rows, u_cols = requests // (n // m), units // m
     asg = assignment.reshape(1, requests)
     dma = pltpu.SemaphoreType.DMA
-    row = lambda a: a.reshape(1, a.shape[0])
+    q_rows = -(-(q_cols // HD * rows) // 16) * 16
 
     qkv, hid = pl.pallas_call(
         functools.partial(project_kernel, n, m),
         out_shape=(
-            jax.ShapeDtypeStruct((rows, q_cols), F32),
+            jax.ShapeDtypeStruct((q_rows, HD), F32),
             jax.ShapeDtypeStruct((u_rows, u_cols), BF16),
         ),
-        in_specs=[VMEM] * 8 + [ANY] * 2,
+        in_specs=[VMEM] * 7 + [HBM] * 2,
         out_specs=(VMEM, VMEM),
         scratch_shapes=[
             pltpu.VMEM((depth, q_cols), BF16),
             pltpu.VMEM((m, depth, u_cols), BF16),
             pltpu.VMEM((requests, 128), F32),
             pltpu.VMEM((n, requests, 128), F32),
-            pltpu.VMEM((n, rows, q_cols), F32),
-            pltpu.VMEM((n, rows, q_cols), F32),
+            pltpu.VMEM((n, q_rows, HD), F32),
+            pltpu.VMEM((n, q_rows, HD), BF16),
+            pltpu.VMEM((n, q_rows, HD), BF16),
             pltpu.VMEM((requests, u_cols), F32),
             pltpu.VMEM((n, u_rows, u_cols), BF16),
             pltpu.VMEM((n, u_rows, u_cols), BF16),
@@ -288,12 +298,12 @@
             dma((n,)), dma((n,)), dma((n,)), dma((n,)), dma((n,)), dma((n,)),
         ],
         compiler_params=pltpu.CompilerParams(
-            collective_id=0, has_side_effects=True, vmem_limit_bytes=24 << 20
+            collective_id=0, has_side_effects=True, vmem_limit_bytes=52 << 20
         ),
         name="project",
     )(
-        hidden_in, row(norm1_gain), row(norm1_bias), row(norm2_gain), row(norm2_bias), asg,
-        row(b_qkv), b_up.reshape(m, 1, u_cols), w_qkv, w_up,
+        hidden_in, norm1_gain, norm1_bias, norm2_gain, norm2_bias, asg,
+        b_up.reshape(m, 1, u_cols), w_qkv, w_up,
     )
 
     freq = np.zeros((1, HD), np.float32)
@@ -306,44 +316,40 @@
             jax.ShapeDtypeStruct(key_cache.shape, BF16),
             jax.ShapeDtypeStruct(value_cache.shape, BF16),
         ),
-        in_specs=[SMEM, SMEM, VMEM, VMEM, ANY, ANY],
+        in_specs=[SMEM, SMEM, VMEM, VMEM, VMEM, VMEM, VMEM],
         out_specs=(VMEM, ANY, ANY),
         scratch_shapes=[
-            pltpu.VMEM((rows, heads, span, HD), BF16),
-            pltpu.VMEM((rows, heads, span, HD), BF16),
             pltpu.VMEM((padded, HD), F32),
             pltpu.VMEM((padded, HD), F32),
             pltpu.VMEM((padded, HD), F32),
             pltpu.VMEM((padded, span), F32),
             pltpu.VMEM((padded, HD), F32),
+            pltpu.VMEM((2, rows, heads, 16, HD), BF16),
             dma((2 * rows,)),
             dma((2 * rows,)),
         ],
         compiler_params=pltpu.CompilerParams(vmem_limit_bytes=20 << 20),
         name="attend",
-    )(lengths, assignment, qkv, jnp.asarray(freq), key_cache, value_cache)
+    )(lengths, assignment, qkv, b_qkv.reshape(q_cols // HD, HD), jnp.asarray(freq), key_cache, value_cache)
 
     hidden_out = pl.pallas_call(
         functools.partial(output_kernel, n, m, ny),
         out_shape=jax.ShapeDtypeStruct((requests, depth), BF16),
-        in_specs=[VMEM] * 6 + [ANY] * 2,
+        in_specs=[VMEM] * 8,
         out_specs=VMEM,
         scratch_shapes=[
-            pltpu.VMEM(w_out.shape, BF16),
-            pltpu.VMEM(w_down.shape, BF16),
             pltpu.VMEM((n, u_rows, u_cols), BF16),
             pltpu.VMEM((n, rows, heads * HD), F32),
             pltpu.VMEM((requests, heads * HD), F32),
-            pltpu.VMEM((requests, depth), F32),
-            pltpu.VMEM((ny, requests, depth), F32),
-            dma((2,)),
+            pltpu.VMEM((requests, depth), BF16),
+            pltpu.VMEM((ny, requests, depth), BF16),
             dma((n,)), dma((n,)), dma((n,)), dma((n,)), dma((ny,)), dma((ny,)),
         ],
         compiler_params=pltpu.CompilerParams(
             collective_id=1, has_side_effects=True, vmem_limit_bytes=20 << 20
         ),
         name="output",
-    )(att, hid, hidden_in, asg, row(b_out), row(b_down), w_out, w_down)
+    )(att, hid, hidden_in, asg, b_out, b_down, w_out, w_down)
     return (hidden_out, new_keys, new_values)
 
 

time: 54.4 us -> 44.1 us (0.81)
  local copies, waits for them, and re-layouts: 11.5 us -> 6.05 us
  Pallas kernels: 41.6 us -> 36.9 us
    pallas_call x1, Pallas kernels: 22.5 us -> 18.6 us  [on_device(): pl.pallas_call(functools.partial(project_kernel, n, m), out_shape=(jax.Sh...]
    reshape x7 -> x0, local copies, waits for them, and re-layouts: 3.49 us -> none  [on_device(): row = lambda a: a.reshape(1, a.shape[0])]
    unnamed x27 -> x33, local copies, waits for them, and re-layouts: 8.01 us -> 6.05 us
    pallas_call x1, Pallas kernels: 12.9 us -> 11.9 us  [on_device(): pl.pallas_call(functools.partial(output_kernel, n, m, ny), out_shape=jax....]
where the time goes in v2:
time: 44.1 us; the launch traced here: 43.7 us
  Pallas kernels  36.9 us (84%)
  local copies, waits for them, and re-layouts  6.05 us (14%)
  between operations  0.77 us (2%)
    pallas_call x1, Pallas kernels, on_device(): pl.pallas_call(functools.partial(project_kernel, n, m), out_shape=(jax.Sh...  18.6 us
    pallas_call x1, Pallas kernels, on_device(): pl.pallas_call(functools.partial(output_kernel, n, m, ny), out_shape=jax....  11.9 us
    pallas_call x1, Pallas kernels, on_device(): pl.pallas_call(attend_kernel, out_shape=(jax.ShapeDtypeStruct((rows, head...  6.39 us
    unnamed x33, local copies, waits for them, and re-layouts  6.05 us

profile of v2, /device:TPU:0, one launch (start us, length us, event | category | flops | bytes accessed | tf_op | source)
XLA Modules:
  0.0 43.7 jit_solution(15345624557441583623)
XLA Ops:
  0.6 0.0 copy-start.4
  0.6 0.7 %copy-done.4 = bf16[16,640]{1,0:T(8,128)(2,1)S(1)} copy-done((bf16[16,640]{1,0:T(8,128)(2,1)S(1)}, bf16[16,640]{1,0:T(8,128)(2,1)}, u32[]{:S(2)}) %copy-start.4) | copy-done | bytes 20504
  1.4 0.0 copy-start.5
  1.4 0.7 %copy-done.5 = f32[5120]{0:T(1024)S(1)} copy-done((f32[5120]{0:T(1024)S(1)}, f32[5120]{0:T(1024)}, u32[]{:S(2)}) %copy-start.5) | copy-done | bytes 20504
  2.1 0.0 copy-start.7
  2.1 0.7 %copy-done.7 = s32[16]{0:T(128)S(1)} copy-done((s32[16]{0:T(128)S(1)}, s32[16]{0:T(128)}, u32[]{:S(2)}) %copy-start.7) | copy-done | bytes 88
  2.7 0.0 copy-start.8
  2.8 0.7 %copy-done.8 = f32[640]{0:T(1024)S(1)} copy-done((f32[640]{0:T(1024)S(1)}, f32[640]{0:T(1024)}, u32[]{:S(2)}) %copy-start.8) | copy-done | bytes 2584
  3.4 0.0 copy-start.9
  3.4 0.7 %copy-done.9 = f32[640]{0:T(1024)S(1)} copy-done((f32[640]{0:T(1024)S(1)}, f32[640]{0:T(1024)}, u32[]{:S(2)}) %copy-start.9) | copy-done | bytes 2584
  4.1 0.0 copy-start.10
  4.1 0.7 %copy-done.10 = f32[640]{0:T(1024)S(1)} copy-done((f32[640]{0:T(1024)S(1)}, f32[640]{0:T(1024)}, u32[]{:S(2)}) %copy-start.10) | copy-done | bytes 2584
  4.8 0.0 copy-start.11
  4.8 0.7 %copy-done.11 = f32[640]{0:T(1024)S(1)} copy-done((f32[640]{0:T(1024)S(1)}, f32[640]{0:T(1024)}, u32[]{:S(2)}) %copy-start.11) | copy-done | bytes 2584
  5.5 0.0 copy-start.1
  5.5 0.0 copy-start.2
  5.5 0.0 copy-start.6
  5.5 0.0 copy-start.14
  5.5 0.0 copy-start.15
  5.5 18.6 %project.1 = (f32[64,128]{1,0:T(8,128)S(1)}, bf16[16,640]{1,0:T(8,128)(2,1)S(1)}) custom-call(bf16[16,640]{1,0:T(8,128)(2,1)S(1)} %copy-done.4, f32[640]{0:T(1024)S(1)} %copy-done.8, f32[640]{0:T(1024)S(1)} %copy-done.9, f32[640]{0:T(1024)S(1)} %copy-done.10, f32[640]{0:T(1024)S(1)} %copy-done.11, s32[1,16]{1,0:T(1,128)S(1)} %bitcast.5, ...), custom_call_target="tpu_custom_call" | custom-call | tf_op jit(solution)/shard_map/project/pallas_call | solution.py:278
  24.1 0.0 copy-done.1
  24.1 0.0 copy-done.2
  24.2 0.0 copy-done.6
  24.2 0.0 copy-done.14
  24.2 0.0 copy-done.15
  24.2 0.0 copy-start
  24.2 0.0 copy-start.3
  24.2 0.0 copy-start.12
  24.2 0.0 copy-start.13
  24.2 6.4 %attend.1 = (f32[2,1280]{1,0:T(2,128)S(1)}, bf16[2,10,1024,128]{3,2,1,0:T(8,128)(2,1)}, bf16[2,10,1024,128]{3,2,1,0:T(8,128)(2,1)}) custom-call(s32[16]{0:T(128)S(1)} %copy-done.14, s32[16]{0:T(128)S(1)} %copy-done.7, f32[64,128]{1,0:T(8,128)S(1)} %get-tuple-element.8.qkv_ref, f32[30,128]{1,0:T(8,128)S(1)} %bitcast.4, f32[1,128]{1,0:T(1,128)S(1)} %copy-done.15, ...), custom_call_target="tpu_custom_call" | custom-call | tf_op jit(solution)/shard_map/attend/pallas_call | solution.py:312
  30.6 0.0 copy-done
  30.6 0.5 %copy-done.3 = bf16[1280,640]{1,0:T(8,128)(2,1)S(1)} copy-done((bf16[1280,640]{1,0:T(8,128)(2,1)S(1)}, bf16[1280,640]{1,0:T(8,128)(2,1)}, u32[]{:S(2)}) %copy-start.3) | copy-done | bytes 1638424
  31.2 0.0 copy-done.12
  31.2 0.0 copy-done.13
  31.2 11.9 %output.1 = bf16[16,640]{1,0:T(8,128)(2,1)S(1)} custom-call(f32[2,1280]{1,0:T(2,128)S(1)} %get-tuple-element.9.att_ref, bf16[16,640]{1,0:T(8,128)(2,1)S(1)} %get-tuple-element.10.hid_ref, bf16[16,640]{1,0:T(8,128)(2,1)S(1)} %copy-done.4, s32[1,16]{1,0:T(1,128)S(1)} %bitcast.6, f32[640]{0:T(1024)S(1)} %copy-done.12, f32[640]{0:T(1024)S(1)} %copy-done.13, ...), custom_call_target="tpu_custom_call" | custom-call | tf_op jit(solution)/shard_map/output/pallas_call | solution.py:335
  43.1 0.6 %copy.22 = bf16[16,640]{1,0:T(8,128)(2,1)} copy(bf16[16,640]{1,0:T(8,128)(2,1)S(1)} %output.1) | data formatting | bytes 40960
Async XLA Ops:
  0.6 0.7 %copy-start.4 = (bf16[16,640]{1,0:T(8,128)(2,1)S(1)}, bf16[16,640]{1,0:T(8,128)(2,1)}, u32[]{:S(2)}) copy-start(bf16[16,640]{1,0:T(8,128)(2,1)} %h_ref.3) | copy-start | bytes 61444
  1.4 0.7 %copy-start.5 = (f32[5120]{0:T(1024)S(1)}, f32[5120]{0:T(1024)}, u32[]{:S(2)}) copy-start(f32[5120]{0:T(1024)} %param.28) | copy-start | bytes 61444
  2.1 0.7 %copy-start.7 = (s32[16]{0:T(128)S(1)}, s32[16]{0:T(128)}, u32[]{:S(2)}) copy-start(s32[16]{0:T(128)} %asg_ref.1) | copy-start | bytes 196
  2.7 0.7 %copy-start.8 = (f32[640]{0:T(1024)S(1)}, f32[640]{0:T(1024)}, u32[]{:S(2)}) copy-start(f32[640]{0:T(1024)} %g1_ref.1) | copy-start | bytes 7684
  3.4 0.7 %copy-start.9 = (f32[640]{0:T(1024)S(1)}, f32[640]{0:T(1024)}, u32[]{:S(2)}) copy-start(f32[640]{0:T(1024)} %b1_ref.1) | copy-start | bytes 7684
  4.1 0.7 %copy-start.10 = (f32[640]{0:T(1024)S(1)}, f32[640]{0:T(1024)}, u32[]{:S(2)}) copy-start(f32[640]{0:T(1024)} %g2_ref.1) | copy-start | bytes 7684
  4.8 0.7 %copy-start.11 = (f32[640]{0:T(1024)S(1)}, f32[640]{0:T(1024)}, u32[]{:S(2)}) copy-start(f32[640]{0:T(1024)} %b2_ref.1) | copy-start | bytes 7684
  5.5 18.6 %copy-start.1 = (bf16[2,10,1024,128]{3,2,1,0:T(8,128)(2,1)S(1)}, bf16[2,10,1024,128]{3,2,1,0:T(8,128)(2,1)}, u32[]{:S(2)}) copy-start(bf16[2,10,1024,128]{3,2,1,0:T(8,128)(2,1)} %kbuf.1) | copy-start | bytes 15728644
  5.5 18.7 %copy-start.2 = (bf16[2,10,1024,128]{3,2,1,0:T(8,128)(2,1)S(1)}, bf16[2,10,1024,128]{3,2,1,0:T(8,128)(2,1)}, u32[]{:S(2)}) copy-start(bf16[2,10,1024,128]{3,2,1,0:T(8,128)(2,1)} %vbuf.1) | copy-start | bytes 15728644
  5.5 18.7 %copy-start.6 = (f32[3840]{0:T(1024)S(1)}, f32[3840]{0:T(1024)}, u32[]{:S(2)}) copy-start(f32[3840]{0:T(1024)} %param.24) | copy-start | bytes 46084
  5.5 18.7 %copy-start.14 = (s32[16]{0:T(128)S(1)}, s32[16]{0:T(128)}, u32[]{:S(2)}) copy-start(s32[16]{0:T(128)} %len_ref.1) | copy-start | bytes 196
  5.5 18.7 %copy-start.15 = (f32[1,128]{1,0:T(1,128)S(1)}, f32[1,128]{1,0:T(1,128)}, u32[]{:S(2)}) copy-start(f32[1,128]{1,0:T(1,128)} %constant.2.clone.freq_ref) | copy-start | bytes 1540
  24.2 6.4 %copy-start = (bf16[5120,640]{1,0:T(8,128)(2,1)S(1)}, bf16[5120,640]{1,0:T(8,128)(2,1)}, u32[]{:S(2)}) copy-start(bf16[5120,640]{1,0:T(8,128)(2,1)} %wd.1) | copy-start | bytes 19660804
  24.2 7.0 %copy-start.3 = (bf16[1280,640]{1,0:T(8,128)(2,1)S(1)}, bf16[1280,640]{1,0:T(8,128)(2,1)}, u32[]{:S(2)}) copy-start(bf16[1280,640]{1,0:T(8,128)(2,1)} %wo.1) | copy-start | bytes 4915204
  24.2 7.0 %copy-start.12 = (f32[640]{0:T(1024)S(1)}, f32[640]{0:T(1024)}, u32[]{:S(2)}) copy-start(f32[640]{0:T(1024)} %bo_ref.1) | copy-start | bytes 7684
  24.2 7.0 %copy-start.13 = (f32[640]{0:T(1024)S(1)}, f32[640]{0:T(1024)}, u32[]{:S(2)}) copy-start(f32[640]{0:T(1024)} %bd_ref.1) | copy-start | bytes 7684

commit v3 on v2

--- a/solution.py
+++ b/solution.py
@@ -35,8 +35,9 @@
 
 
 def project_kernel(
-    n, m, h_ref, g1_ref, b1_ref, g2_ref, b2_ref, asg_ref, bu_ref, wq_hbm, wu_hbm,
+    n, m, h_hbm, g1_hbm, b1_hbm, g2_hbm, b2_hbm, asg_hbm, bu_hbm, wq_hbm, wu_hbm,
     qkv_ref, hid_ref,
+    h_ref, g1_ref, b1_ref, g2_ref, b2_ref, asg_ref, bu_ref, small_sem,
     wq, wu, st_own, st_in, q_wide, q_send, q_in, u_part, u_send, u_in,
     wsem, s_ssem, s_rsem, q_ssem, q_rsem, u_ssem, u_rsem,
 ):
@@ -47,6 +48,13 @@
     tiles = wq.shape[1] // HD
     u_rows, u_cols = u_send.shape[1:]
     my_col, my_group = lax.rem(me, m), me // m
+    pairs = (
+        (asg_hbm, asg_ref), (h_hbm, h_ref), (g1_hbm, g1_ref), (b1_hbm, b1_ref),
+        (g2_hbm, g2_ref), (b2_hbm, b2_ref), (bu_hbm, bu_ref),
+    )
+    small = [pltpu.make_async_copy(a, b, small_sem.at[i]) for i, (a, b) in enumerate(pairs)]
+    for copy in small:
+        copy.start()
     load_q = pltpu.make_async_copy(wq_hbm, wq, wsem.at[m])
     load_q.start()
     order = list(range(1, m)) + [0]
@@ -61,6 +69,8 @@
     for k in range(1, n):
         pl.semaphore_signal(barrier, inc=1, device_id={"gx": lax.rem(me + k, n)}, device_id_type=MESH)
 
+    for copy in small:
+        copy.wait()
     place = slot_rows(asg_ref)
     x = jnp.dot(place, h_ref[...], preferred_element_type=F32)
     sums = jnp.sum(x, axis=1, keepdims=True)
@@ -281,9 +291,17 @@
             jax.ShapeDtypeStruct((q_rows, HD), F32),
             jax.ShapeDtypeStruct((u_rows, u_cols), BF16),
         ),
-        in_specs=[VMEM] * 7 + [HBM] * 2,
+        in_specs=[HBM] * 9,
         out_specs=(VMEM, VMEM),
         scratch_shapes=[
+            pltpu.VMEM((requests, depth), BF16),
+            pltpu.VMEM((depth,), F32),
+            pltpu.VMEM((depth,), F32),
+            pltpu.VMEM((depth,), F32),
+            pltpu.VMEM((depth,), F32),
+            pltpu.VMEM((1, requests), jnp.int32),
+            pltpu.VMEM((m, 1, u_cols), F32),
+            dma((7,)),
             pltpu.VMEM((depth, q_cols), BF16),
             pltpu.VMEM((m, depth, u_cols), BF16),
             pltpu.VMEM((requests, 128), F32),
@@ -298,7 +316,7 @@
             dma((n,)), dma((n,)), dma((n,)), dma((n,)), dma((n,)), dma((n,)),
         ],
         compiler_params=pltpu.CompilerParams(
-            collective_id=0, has_side_effects=True, vmem_limit_bytes=52 << 20
+            collective_id=0, has_side_effects=True, vmem_limit_bytes=(54 << 20) - (60 << 10)
         ),
         name="project",
     )(

time: 44.1 us -> 45.4 us (1.029)
  Pallas kernels: 36.9 us -> 40 us
  local copies, waits for them, and re-layouts: 6.05 us -> 4.45 us
    pallas_call x1, Pallas kernels: 18.6 us -> 20.6 us  [on_device(): pl.pallas_call(functools.partial(project_kernel, n, m), out_shape=(jax.Sh...]
    unnamed x33 -> x27, local copies, waits for them, and re-layouts: 6.05 us -> 4.45 us
    pallas_call x1, Pallas kernels: 11.9 us -> 12.9 us  [on_device(): pl.pallas_call(functools.partial(output_kernel, n, m, ny), out_shape=jax....]
where the time goes in v3:
time: 45.4 us; the launch traced here: 45.2 us
  Pallas kernels  40 us (88%)
  local copies, waits for them, and re-layouts  4.45 us (10%)
  between operations  0.78 us (2%)
    pallas_call x1, Pallas kernels, on_device(): pl.pallas_call(functools.partial(project_kernel, n, m), out_shape=(jax.Sh...  20.6 us
    pallas_call x1, Pallas kernels, on_device(): pl.pallas_call(functools.partial(output_kernel, n, m, ny), out_shape=jax....  12.9 us
    pallas_call x1, Pallas kernels, on_device(): pl.pallas_call(attend_kernel, out_shape=(jax.ShapeDtypeStruct((rows, head...  6.39 us
    unnamed x27, local copies, waits for them, and re-layouts  4.45 us

profile of v3, /device:TPU:0, one launch (start us, length us, event | category | flops | bytes accessed | tf_op | source)
XLA Modules:
  0.0 45.2 jit_solution(17795860981724019487)
XLA Ops:
  0.6 0.0 copy-start.1
  0.6 0.0 copy-start.7
  0.7 0.0 copy-start.8
  0.7 0.0 copy-start.11
  0.7 0.0 copy-start.12
  0.7 20.6 %project.1 = (f32[64,128]{1,0:T(8,128)}, bf16[16,640]{1,0:T(8,128)(2,1)}) custom-call(bf16[16,640]{1,0:T(8,128)(2,1)} %h_ref.1, f32[640]{0:T(1024)} %g1_hbm.1, f32[640]{0:T(1024)} %b1_hbm.1, f32[640]{0:T(1024)} %g2_hbm.1, f32[640]{0:T(1024)} %b2_hbm.1, s32[1,16]{1,0:T(1,128)} %bitcast.4, f32[8,1,640]{2,1,0:T(1,128)} %bitcast.6, bf16[640,3840]{1,0:T(8,128)(2,1)} %wq_hbm.1, ...), custom_call_target="tpu_custom_call" | custom-call | tf_op jit(solution)/shard_map/project/pallas_call | solution.py:288
  21.3 0.0 copy-done.1
  21.3 0.0 copy-done.7
  21.4 0.0 copy-done.8
  21.4 0.0 copy-done.11
  21.4 0.0 copy-done.12
  21.4 0.0 copy-start.2
  21.4 2.5 %copy-done.2 = bf16[2,10,1024,128]{3,2,1,0:T(8,128)(2,1)S(1)} copy-done((bf16[2,10,1024,128]{3,2,1,0:T(8,128)(2,1)S(1)}, bf16[2,10,1024,128]{3,2,1,0:T(8,128)(2,1)}, u32[]{:S(2)}) %copy-start.2) | copy-done | bytes 5242904
  23.9 0.0 copy-start.5
  23.9 0.8 %copy-done.5 = f32[64,128]{1,0:T(8,128)S(1)} copy-done((f32[64,128]{1,0:T(8,128)S(1)}, f32[64,128]{1,0:T(8,128)}, u32[]{:S(2)}) %copy-start.5) | copy-done | bytes 32792
  24.6 0.0 copy-start
  24.6 0.0 copy-start.3
  24.6 0.0 copy-start.4
  24.6 0.0 copy-start.6
  24.6 0.0 copy-start.9
  24.7 0.0 copy-start.10
  24.7 6.4 %attend.1 = (f32[2,1280]{1,0:T(2,128)S(1)}, bf16[2,10,1024,128]{3,2,1,0:T(8,128)(2,1)}, bf16[2,10,1024,128]{3,2,1,0:T(8,128)(2,1)}) custom-call(s32[16]{0:T(128)S(1)} %copy-done.11, s32[16]{0:T(128)S(1)} %copy-done.8, f32[64,128]{1,0:T(8,128)S(1)} %copy-done.5, f32[30,128]{1,0:T(8,128)S(1)} %bitcast.3, f32[1,128]{1,0:T(1,128)S(1)} %copy-done.12, ...), custom_call_target="tpu_custom_call" | custom-call | tf_op jit(solution)/shard_map/attend/pallas_call | solution.py:330
  31.1 0.0 copy-done
  31.1 0.6 %copy-done.3 = bf16[1280,640]{1,0:T(8,128)(2,1)S(1)} copy-done((bf16[1280,640]{1,0:T(8,128)(2,1)S(1)}, bf16[1280,640]{1,0:T(8,128)(2,1)}, u32[]{:S(2)}) %copy-start.3) | copy-done | bytes 1638424
  31.6 0.0 copy-done.4
  31.6 0.0 copy-done.6
  31.6 0.0 copy-done.9
  31.6 0.0 copy-done.10
  31.6 12.9 %output.1 = bf16[16,640]{1,0:T(8,128)(2,1)S(1)} custom-call(f32[2,1280]{1,0:T(2,128)S(1)} %get-tuple-element.9.att_ref, bf16[16,640]{1,0:T(8,128)(2,1)S(1)} %copy-done.6, bf16[16,640]{1,0:T(8,128)(2,1)S(1)} %copy-done.4, s32[1,16]{1,0:T(1,128)S(1)} %bitcast.5, f32[640]{0:T(1024)S(1)} %copy-done.9, f32[640]{0:T(1024)S(1)} %copy-done.10, ...), custom_call_target="tpu_custom_call" | custom-call | tf_op jit(solution)/shard_map/output/pallas_call | solution.py:353
  44.6 0.6 %copy.22 = bf16[16,640]{1,0:T(8,128)(2,1)} copy(bf16[16,640]{1,0:T(8,128)(2,1)S(1)} %output.1) | data formatting | bytes 40960
Async XLA Ops:
  0.6 20.7 %copy-start.1 = (bf16[2,10,1024,128]{3,2,1,0:T(8,128)(2,1)S(1)}, bf16[2,10,1024,128]{3,2,1,0:T(8,128)(2,1)}, u32[]{:S(2)}) copy-start(bf16[2,10,1024,128]{3,2,1,0:T(8,128)(2,1)} %kbuf.1) | copy-start | bytes 15728644
  0.6 20.7 %copy-start.7 = (f32[3840]{0:T(1024)S(1)}, f32[3840]{0:T(1024)}, u32[]{:S(2)}) copy-start(f32[3840]{0:T(1024)} %param.24) | copy-start | bytes 46084
  0.7 20.7 %copy-start.8 = (s32[16]{0:T(128)S(1)}, s32[16]{0:T(128)}, u32[]{:S(2)}) copy-start(s32[16]{0:T(128)} %asg_ref.1) | copy-start | bytes 196
  0.7 20.7 %copy-start.11 = (s32[16]{0:T(128)S(1)}, s32[16]{0:T(128)}, u32[]{:S(2)}) copy-start(s32[16]{0:T(128)} %len_ref.1) | copy-start | bytes 196
  0.7 20.7 %copy-start.12 = (f32[1,128]{1,0:T(1,128)S(1)}, f32[1,128]{1,0:T(1,128)}, u32[]{:S(2)}) copy-start(f32[1,128]{1,0:T(1,128)} %constant.2.clone.freq_ref) | copy-start | bytes 1540
  21.4 2.5 %copy-start.2 = (bf16[2,10,1024,128]{3,2,1,0:T(8,128)(2,1)S(1)}, bf16[2,10,1024,128]{3,2,1,0:T(8,128)(2,1)}, u32[]{:S(2)}) copy-start(bf16[2,10,1024,128]{3,2,1,0:T(8,128)(2,1)} %vbuf.1) | copy-start | bytes 15728644
  23.9 0.8 %copy-start.5 = (f32[64,128]{1,0:T(8,128)S(1)}, f32[64,128]{1,0:T(8,128)}, u32[]{:S(2)}) copy-start(f32[64,128]{1,0:T(8,128)} %get-tuple-element.8.qkv_ref) | copy-start | bytes 98308
  24.6 6.4 %copy-start = (bf16[5120,640]{1,0:T(8,128)(2,1)S(1)}, bf16[5120,640]{1,0:T(8,128)(2,1)}, u32[]{:S(2)}) copy-start(bf16[5120,640]{1,0:T(8,128)(2,1)} %wd.1) | copy-start | bytes 19660804
  24.6 7.0 %copy-start.3 = (bf16[1280,640]{1,0:T(8,128)(2,1)S(1)}, bf16[1280,640]{1,0:T(8,128)(2,1)}, u32[]{:S(2)}) copy-start(bf16[1280,640]{1,0:T(8,128)(2,1)} %wo.1) | copy-start | bytes 4915204
  24.6 7.0 %copy-start.4 = (bf16[16,640]{1,0:T(8,128)(2,1)S(1)}, bf16[16,640]{1,0:T(8,128)(2,1)}, u32[]{:S(2)}) copy-start(bf16[16,640]{1,0:T(8,128)(2,1)} %h_ref.1) | copy-start | bytes 61444
  24.6 7.0 %copy-start.6 = (bf16[16,640]{1,0:T(8,128)(2,1)S(1)}, bf16[16,640]{1,0:T(8,128)(2,1)}, u32[]{:S(2)}) copy-start(bf16[16,640]{1,0:T(8,128)(2,1)} %get-tuple-element.10.hid_ref) | copy-start | bytes 61444
  24.6 7.0 %copy-start.9 = (f32[640]{0:T(1024)S(1)}, f32[640]{0:T(1024)}, u32[]{:S(2)}) copy-start(f32[640]{0:T(1024)} %bo_ref.1) | copy-start | bytes 7684
  24.7 7.0 %copy-start.10 = (f32[640]{0:T(1024)S(1)}, f32[640]{0:T(1024)}, u32[]{:S(2)}) copy-start(f32[640]{0:T(1024)} %bd_ref.1) | copy-start | bytes 7684

commit v4 on v2

--- a/solution.py
+++ b/solution.py
@@ -35,7 +35,7 @@
 
 
 def project_kernel(
-    n, m, h_ref, g1_ref, b1_ref, g2_ref, b2_ref, asg_ref, bu_ref, wq_hbm, wu_hbm,
+    n, m, h_ref, vec_ref, asg_ref, bu_ref, wq_hbm, wu_hbm,
     qkv_ref, hid_ref,
     wq, wu, st_own, st_in, q_wide, q_send, q_in, u_part, u_send, u_in,
     wsem, s_ssem, s_rsem, q_ssem, q_rsem, u_ssem, u_rsem,
@@ -80,8 +80,8 @@
     mean = total[:, 0:1] / width
     var = total[:, 1:2] / width - mean * mean
     normed = (x - mean) * lax.rsqrt(var + 1e-05)
-    attn_in = (normed * g1_ref[...].reshape(1, depth) + b1_ref[...].reshape(1, depth)).astype(BF16)
-    mlp_in = (normed * g2_ref[...].reshape(1, depth) + b2_ref[...].reshape(1, depth)).astype(BF16)
+    attn_in = (normed * vec_ref[0:1, :] + vec_ref[1:2, :]).astype(BF16)
+    mlp_in = (normed * vec_ref[2:3, :] + vec_ref[3:4, :]).astype(BF16)
 
     load_q.wait()
     qkv = jnp.dot(attn_in, wq[...], preferred_element_type=F32)
@@ -281,7 +281,7 @@
             jax.ShapeDtypeStruct((q_rows, HD), F32),
             jax.ShapeDtypeStruct((u_rows, u_cols), BF16),
         ),
-        in_specs=[VMEM] * 7 + [HBM] * 2,
+        in_specs=[VMEM] * 4 + [HBM] * 2,
         out_specs=(VMEM, VMEM),
         scratch_shapes=[
             pltpu.VMEM((depth, q_cols), BF16),
@@ -302,7 +302,7 @@
         ),
         name="project",
     )(
-        hidden_in, norm1_gain, norm1_bias, norm2_gain, norm2_bias, asg,
+        hidden_in, jnp.stack([norm1_gain, norm1_bias, norm2_gain, norm2_bias]), asg,
         b_up.reshape(m, 1, u_cols), w_qkv, w_up,
     )
 

time: 44.1 us -> 44.1 us (level)
    another operation x0 -> x4, local copies, waits for them, and re-layouts: none -> 2.76 us  [on_device(): jnp.stack([norm1_gain, norm1_bias, norm2_gain, norm2_bias])]
    unnamed x33 -> x25, local copies, waits for them, and re-layouts: 6.05 us -> 3.31 us
where the time goes in v4:
time: 44.1 us; the launch traced here: 43.7 us
  Pallas kernels  36.9 us (84%)
  local copies, waits for them, and re-layouts  6.06 us (14%)
  between operations  0.76 us (2%)
    pallas_call x1, Pallas kernels, on_device(): pl.pallas_call(functools.partial(project_kernel, n, m), out_shape=(jax.Sh...  18.6 us
    pallas_call x1, Pallas kernels, on_device(): pl.pallas_call(functools.partial(output_kernel, n, m, ny), out_shape=jax....  11.9 us
    pallas_call x1, Pallas kernels, on_device(): pl.pallas_call(attend_kernel, out_shape=(jax.ShapeDtypeStruct((rows, head...  6.39 us
    unnamed x25, local copies, waits for them, and re-layouts  3.31 us
    another operation x4, local copies, waits for them, and re-layouts, on_device(): jnp.stack([norm1_gain, norm1_bias, norm2_gain, norm2_bias])  2.76 us

profile of v4, /device:TPU:0, one launch (start us, length us, event | category | flops | bytes accessed | tf_op | source)
XLA Modules:
  0.0 43.7 jit_solution(543771365964569676)
XLA Ops:
  0.6 0.7 %stack.15 = f32[1,640]{1,0:T(1,128)S(1)} reshape(f32[640]{0:T(1024)} %param.19) | data formatting | bytes 5120 | tf_op jit(solution)/shard_map/stack | solution.py:305
  1.3 0.7 %stack.16 = f32[1,640]{1,0:T(1,128)S(1)} reshape(f32[640]{0:T(1024)} %param.20) | data formatting | bytes 5120 | tf_op jit(solution)/shard_map/stack | solution.py:305
  2.0 0.7 %stack.17 = f32[1,640]{1,0:T(1,128)S(1)} reshape(f32[640]{0:T(1024)} %param.21) | data formatting | bytes 5120 | tf_op jit(solution)/shard_map/stack | solution.py:305
  2.7 0.7 %stack.18 = f32[1,640]{1,0:T(1,128)S(1)} reshape(f32[640]{0:T(1024)} %param.22) | data formatting | bytes 5120 | tf_op jit(solution)/shard_map/stack | solution.py:305
  3.4 0.0 copy-start.4
  3.4 0.7 %copy-done.4 = bf16[16,640]{1,0:T(8,128)(2,1)S(1)} copy-done((bf16[16,640]{1,0:T(8,128)(2,1)S(1)}, bf16[16,640]{1,0:T(8,128)(2,1)}, u32[]{:S(2)}) %copy-start.4) | copy-done | bytes 20504
  4.1 0.0 copy-start.5
  4.1 0.7 %copy-done.5 = f32[5120]{0:T(1024)S(1)} copy-done((f32[5120]{0:T(1024)S(1)}, f32[5120]{0:T(1024)}, u32[]{:S(2)}) %copy-start.5) | copy-done | bytes 20504
  4.9 0.0 copy-start.7
  4.9 0.7 %copy-done.7 = s32[16]{0:T(128)S(1)} copy-done((s32[16]{0:T(128)S(1)}, s32[16]{0:T(128)}, u32[]{:S(2)}) %copy-start.7) | copy-done | bytes 88
  5.5 0.0 copy-start.1
  5.5 0.0 copy-start.2
  5.5 0.0 copy-start.6
  5.5 0.0 copy-start.10
  5.5 0.0 copy-start.11
  5.5 18.6 %project.1 = (f32[64,128]{1,0:T(8,128)S(1)}, bf16[16,640]{1,0:T(8,128)(2,1)S(1)}) custom-call(bf16[16,640]{1,0:T(8,128)(2,1)S(1)} %copy-done.4, f32[4,640]{1,0:T(4,128)S(1)} %pad_maximum_fusion.vec_ref, s32[1,16]{1,0:T(1,128)S(1)} %bitcast.5, f32[8,1,640]{2,1,0:T(1,128)S(1)} %bitcast.3, bf16[640,3840]{1,0:T(8,128)(2,1)} %wq_hbm.1, bf16[640,5120]{1,0:T(8,128)(2,1)} %wu_hbm.1), custom_call_target="tpu_custom_call" | custom-call | tf_op jit(solution)/shard_map/project/pallas_call | solution.py:278
  24.2 0.0 copy-done.1
  24.2 0.0 copy-done.2
  24.2 0.0 copy-done.6
  24.2 0.0 copy-done.10
  24.2 0.0 copy-done.11
  24.2 0.0 copy-start
  24.2 0.0 copy-start.3
  24.2 0.0 copy-start.8
  24.2 0.0 copy-start.9
  24.3 6.4 %attend.1 = (f32[2,1280]{1,0:T(2,128)S(1)}, bf16[2,10,1024,128]{3,2,1,0:T(8,128)(2,1)}, bf16[2,10,1024,128]{3,2,1,0:T(8,128)(2,1)}) custom-call(s32[16]{0:T(128)S(1)} %copy-done.10, s32[16]{0:T(128)S(1)} %copy-done.7, f32[64,128]{1,0:T(8,128)S(1)} %get-tuple-element.8.qkv_ref, f32[30,128]{1,0:T(8,128)S(1)} %bitcast.4, f32[1,128]{1,0:T(1,128)S(1)} %copy-done.11, ...), custom_call_target="tpu_custom_call" | custom-call | tf_op jit(solution)/shard_map/attend/pallas_call | solution.py:312
  30.7 0.0 copy-done
  30.7 0.5 %copy-done.3 = bf16[1280,640]{1,0:T(8,128)(2,1)S(1)} copy-done((bf16[1280,640]{1,0:T(8,128)(2,1)S(1)}, bf16[1280,640]{1,0:T(8,128)(2,1)}, u32[]{:S(2)}) %copy-start.3) | copy-done | bytes 1638424
  31.2 0.0 copy-done.8
  31.2 0.0 copy-done.9
  31.2 11.9 %output.1 = bf16[16,640]{1,0:T(8,128)(2,1)S(1)} custom-call(f32[2,1280]{1,0:T(2,128)S(1)} %get-tuple-element.9.att_ref, bf16[16,640]{1,0:T(8,128)(2,1)S(1)} %get-tuple-element.10.hid_ref, bf16[16,640]{1,0:T(8,128)(2,1)S(1)} %copy-done.4, s32[1,16]{1,0:T(1,128)S(1)} %bitcast.6, f32[640]{0:T(1024)S(1)} %copy-done.8, f32[640]{0:T(1024)S(1)} %copy-done.9, ...), custom_call_target="tpu_custom_call" | custom-call | tf_op jit(solution)/shard_map/output/pallas_call | solution.py:335
  43.1 0.6 %copy.22 = bf16[16,640]{1,0:T(8,128)(2,1)} copy(bf16[16,640]{1,0:T(8,128)(2,1)S(1)} %output.1) | data formatting | bytes 40960
  (1 shorter events, 0.0 us)
Async XLA Ops:
  3.4 0.7 %copy-start.4 = (bf16[16,640]{1,0:T(8,128)(2,1)S(1)}, bf16[16,640]{1,0:T(8,128)(2,1)}, u32[]{:S(2)}) copy-start(bf16[16,640]{1,0:T(8,128)(2,1)} %h_ref.3) | copy-start | bytes 61444
  4.1 0.7 %copy-start.5 = (f32[5120]{0:T(1024)S(1)}, f32[5120]{0:T(1024)}, u32[]{:S(2)}) copy-start(f32[5120]{0:T(1024)} %param.28) | copy-start | bytes 61444
  4.9 0.7 %copy-start.7 = (s32[16]{0:T(128)S(1)}, s32[16]{0:T(128)}, u32[]{:S(2)}) copy-start(s32[16]{0:T(128)} %asg_ref.1) | copy-start | bytes 196
  5.5 18.6 %copy-start.1 = (bf16[2,10,1024,128]{3,2,1,0:T(8,128)(2,1)S(1)}, bf16[2,10,1024,128]{3,2,1,0:T(8,128)(2,1)}, u32[]{:S(2)}) copy-start(bf16[2,10,1024,128]{3,2,1,0:T(8,128)(2,1)} %kbuf.1) | copy-start | bytes 15728644
  5.5 18.6 %copy-start.2 = (bf16[2,10,1024,128]{3,2,1,0:T(8,128)(2,1)S(1)}, bf16[2,10,1024,128]{3,2,1,0:T(8,128)(2,1)}, u32[]{:S(2)}) copy-start(bf16[2,10,1024,128]{3,2,1,0:T(8,128)(2,1)} %vbuf.1) | copy-start | bytes 15728644
  5.5 18.7 %copy-start.6 = (f32[3840]{0:T(1024)S(1)}, f32[3840]{0:T(1024)}, u32[]{:S(2)}) copy-start(f32[3840]{0:T(1024)} %param.24) | copy-start | bytes 46084
  5.5 18.7 %copy-start.10 = (s32[16]{0:T(128)S(1)}, s32[16]{0:T(128)}, u32[]{:S(2)}) copy-start(s32[16]{0:T(128)} %len_ref.1) | copy-start | bytes 196
  5.5 18.7 %copy-start.11 = (f32[1,128]{1,0:T(1,128)S(1)}, f32[1,128]{1,0:T(1,128)}, u32[]{:S(2)}) copy-start(f32[1,128]{1,0:T(1,128)} %constant.2.clone.freq_ref) | copy-start | bytes 1540
  24.2 6.4 %copy-start = (bf16[5120,640]{1,0:T(8,128)(2,1)S(1)}, bf16[5120,640]{1,0:T(8,128)(2,1)}, u32[]{:S(2)}) copy-start(bf16[5120,640]{1,0:T(8,128)(2,1)} %wd.1) | copy-start | bytes 19660804
  24.2 7.0 %copy-start.3 = (bf16[1280,640]{1,0:T(8,128)(2,1)S(1)}, bf16[1280,640]{1,0:T(8,128)(2,1)}, u32[]{:S(2)}) copy-start(bf16[1280,640]{1,0:T(8,128)(2,1)} %wo.1) | copy-start | bytes 4915204
  24.2 7.0 %copy-start.8 = (f32[640]{0:T(1024)S(1)}, f32[640]{0:T(1024)}, u32[]{:S(2)}) copy-start(f32[640]{0:T(1024)} %bo_ref.1) | copy-start | bytes 7684
  24.2 7.0 %copy-start.9 = (f32[640]{0:T(1024)S(1)}, f32[640]{0:T(1024)}, u32[]{:S(2)}) copy-start(f32[640]{0:T(1024)} %bd_ref.1) | copy-start | bytes 7684
